TPU v7x, 256 devices: a whole 4x4x8 slice. The times are simulated.
256 devices in a mesh: ctx: 32 (over z_hi, x, y), head: 8 (over z_lo, core).
Axes of the slice: x: 4, y: 4, z: 8 (z_hi: 2, z_lo: 4; z = z_hi * 4 + z_lo), core: 2. Of those that a mesh axis runs over, the one named last changes fastest.
Arguments:
- queries: bfloat16 [2, 8192, 4096], P(None, 'ctx', 'head'), may hold values from -6 to 6
- keys: bfloat16 [2, 8192, 4096], P(None, 'ctx', 'head'), may hold values from -6 to 6
- values: bfloat16 [2, 8192, 4096], P(None, 'ctx', 'head'), may hold values from -6 to 6
- token_gate: float32 [2, 32, 8192], P(None, 'head', 'ctx'), may hold values from 0.2 to 1
- head_rate: float32 [32], P('head'), may hold values from 2.861023e-07 to 0.001953125
- init_state: float32 [32, 128, 128], P('head'), may hold values from -0.53033006 to 0.53033006
- norm_gain: float32 [4096], P('head'), may hold values from 0.5 to 1.5
- out_proj: bfloat16 [4096, 4096], P('head'), may hold values from -0.09375 to 0.09375
- plan: int32 [2], replicated, may hold values from 0 to 1, each once
Outputs:
- layer_out: bfloat16 [8192, 2, 4096], P(('ctx', 'head'))
Inputs may be any that keep to these rules, and one draw needn't show every extreme that they name: `plan`: each sequence appears exactly once.
All inputs are finite; a program needn't handle non-finite values.
Results may differ from a plain program's by a relative error of at most 0.0049.
Values sent between devices are 32-bit elements; how exact they have to be, the bound alone decides.
A program may use at most 64 MiB of HBM per device.

v0:
```python
import jax
import jax.numpy as jnp
from jax import lax
from jax.sharding import PartitionSpec as P

HS = 128
MB = 64


EPS = 1e-06


def passed_along(block, axis, distance):
    devices = range(lax.axis_size(axis))
    route = [(i - distance, i) for i in devices if i - distance in devices]
    return lax.ppermute(block, axis, route)


def matmul_state(left, right):
    return jnp.einsum("shij,shjk->shik", left, right, precision=lax.Precision.HIGHEST)


def compose(earlier, later):
    return (matmul_state(later[0], earlier[0]), matmul_state(later[0], earlier[1]) + later[1])


def per_device(queries, keys, values, token_gate, head_rate, init_state, norm_gain, out_proj, plan):
    best = lax.Precision.HIGHEST
    seqs, rows = (queries.shape[0], queries.shape[1])
    heads_here = init_state.shape[0]
    blocks = rows // MB

    def split(arr):
        arr = jnp.take(arr, plan, axis=0).astype(jnp.float32)
        arr = arr.reshape(seqs, blocks, MB, heads_here, HS)
        return jnp.transpose(arr, (1, 0, 3, 2, 4))

    qb, kb, vb = (split(queries), split(keys), split(values))
    gates = jnp.take(token_gate, plan, axis=0) * head_rate[None, :, None]
    eb = jnp.transpose(gates.reshape(seqs, heads_here, blocks, MB), (2, 0, 1, 3))
    eye = jnp.broadcast_to(jnp.eye(HS, dtype=jnp.float32), (seqs, heads_here, HS, HS))
    zero_state = jnp.zeros((seqs, heads_here, HS, HS), jnp.float32)

    def map_step(carry, blk):
        km, vm, em = blk
        weighted = km * em[..., None]
        factor = eye - jnp.einsum("shmi,shmj->shij", weighted, km, precision=best)
        drive = jnp.einsum("shmi,shmj->shij", weighted, vm, precision=best)
        return (compose(carry, (factor, drive)), None)

    (slab_factor, slab_drive), _ = lax.scan(map_step, (eye, zero_state), (kb, vb, eb))
    start = jnp.broadcast_to(init_state[None], (seqs, heads_here, HS, HS))
    position = lax.axis_index("ctx")

    def turn(count, state):
        advanced = matmul_state(slab_factor, state) + slab_drive
        moved = passed_along(advanced, "ctx", 1)
        return jnp.where(position == 0, start, moved)

    entering = lax.fori_loop(0, lax.axis_size("ctx") - 1, turn, start)
    lower = jnp.arange(MB)[:, None] >= jnp.arange(MB)[None, :]

    def out_step(weights, blk):
        qm, km, vm, em = blk
        err = jnp.einsum("shmi,shij->shmj", km, weights, precision=best) - vm
        qw = jnp.einsum("shmi,shij->shmj", qm, weights, precision=best)
        scores = jnp.einsum("shmi,shni->shmn", qm, km, precision=best) * em[:, :, None, :]
        scores = jnp.where(lower[None, None], scores, 0.0)
        zout = qw - jnp.einsum("shmn,shnj->shmj", scores, err, precision=best)
        weights = weights - jnp.einsum("shmi,shmj->shij", km * em[..., None], err, precision=best)
        return (weights, zout)

    _, zall = lax.scan(out_step, entering, (qb, kb, vb, eb))
    scale = lax.rsqrt(jnp.mean(zall * zall, axis=-1, keepdims=True) + EPS)
    gain = norm_gain.reshape(heads_here, HS)
    normed = (zall * scale * gain[None, None, :, None, :]).astype(jnp.bfloat16)
    normed = jnp.transpose(normed, (0, 3, 1, 2, 4)).reshape(rows, seqs, heads_here * HS)
    count = lax.axis_size("head") * (rows // lax.axis_size("head"))
    product = jnp.dot(
        normed.reshape(count * seqs, heads_here * HS), out_proj, preferred_element_type=jnp.float32
    )
    summed = lax.psum_scatter(
        product.reshape(count, seqs, out_proj.shape[1]), "head", scatter_dimension=0, tiled=True
    )
    return summed.astype(jnp.bfloat16)


def solution(mesh):
    return jax.shard_map(
        per_device,
        mesh=mesh,
        in_specs=(
            P(None, "ctx", "head"),
            P(None, "ctx", "head"),
            P(None, "ctx", "head"),
            P(None, "head", "ctx"),
            P("head"),
            P("head", None, None),
            P("head"),
            P("head", None),
            P(),
        ),
        out_specs=P(("ctx", "head"), None, None),
        check_vma=False,
    )
```

profile of v0, /device:TPU:166, one launch (start us, length us, event | category | flops | bytes accessed | tf_op | source)
XLA Modules:
  0.0 1108.8 jit_solution(7921345908541304423)
XLA Ops:
  11.4 2.4 gather_fusion.2
  13.9 2.4 gather_fusion.1
  16.3 2.7 select_convert_fusion
  18.9 2.5 reshape.50
  22.8 2.4 copy.13
  25.8 18.4 %while.41 = (s32[]{:T(128)}, f32[2,4,128,128]{3,2,1,0:T(8,128)S(1)}, f32[2,4,128,128]{3,2,1,0:T(8,128)S(1)}, f32[4,2,4,64,128]{4,3,2,1,0:T(8,128)S(1)}, f32[4,2,...) while((s32[]{:T(128)}, ...), condition=%wide.region_1.3_spmd.clone, body=%wide.region_0.0_spmd.clone.sunk | while | flops 604504064 | bytes 7944307 | solution.py:51
  27.0 2.1 fusion.95
  31.6 2.1 fusion.95
  36.2 2.1 fusion.95
  40.8 2.1 fusion.95
  44.2 769.3 %while.39 = (s32[]{:T(128)}, f32[2,4,128,128]{3,2,1,0:T(8,128)S(1)}, pred[]{:T(512)}, f32[2,4,128,128]{3,2,1,0:T(8,128)S(1)}, f32[2,4,128,128]{3,2,1,0:T(8,128)S(1)}, /*index=5*/f32[4,128,128]{2,1,0:T(8,128)S(1)}, s32[]{:T(128)}) while((s32[]{:T(128)}, f32[2,4,128,128]{3,2,1,0:T(8,128)S(1)}, pred[]{:T(512)}, ...), condition=%wide.region_3.5_spmd.clone, body=%wide.region_2.4_spmd.clone.sunk | while | flops 201588736 | bytes 7602322 | solution.py:60
  45.7 3.5 collective-permute-start
  49.1 14.4 %collective-permute-done = f32[2,4,128,128]{3,2,1,0:T(8,128)S(1)} collective-permute-done((f32[2,4,128,128]{3,2,1,0:T(8,128)}, f32[2,4,128,128]{3,2,1,0:T(8,128)S(1)}, u32[]{:S(2)}, u32[]{:S(2)}) %collective-permute-start) | collective-permute-done | bytes 524320 | tf_op jit(solution)/shard_map/while/body/eval_jaxpr/ppermute | solution.py:16
  68.8 15.1 %collective-permute-done = f32[2,4,128,128]{3,2,1,0:T(8,128)S(1)} collective-permute-done((f32[2,4,128,128]{3,2,1,0:T(8,128)}, f32[2,4,128,128]{3,2,1,0:T(8,128)S(1)}, u32[]{:S(2)}, u32[]{:S(2)}) %collective-permute-start) | collective-permute-done | bytes 524320 | tf_op jit(solution)/shard_map/while/body/eval_jaxpr/ppermute | solution.py:16
  89.1 14.2 %collective-permute-done = f32[2,4,128,128]{3,2,1,0:T(8,128)S(1)} collective-permute-done((f32[2,4,128,128]{3,2,1,0:T(8,128)}, f32[2,4,128,128]{3,2,1,0:T(8,128)S(1)}, u32[]{:S(2)}, u32[]{:S(2)}) %collective-permute-start) | collective-permute-done | bytes 524320 | tf_op jit(solution)/shard_map/while/body/eval_jaxpr/ppermute | solution.py:16
  108.5 13.2 %collective-permute-done = f32[2,4,128,128]{3,2,1,0:T(8,128)S(1)} collective-permute-done((f32[2,4,128,128]{3,2,1,0:T(8,128)}, f32[2,4,128,128]{3,2,1,0:T(8,128)S(1)}, u32[]{:S(2)}, u32[]{:S(2)}) %collective-permute-start) | collective-permute-done | bytes 524320 | tf_op jit(solution)/shard_map/while/body/eval_jaxpr/ppermute | solution.py:16
  127.0 12.3 %collective-permute-done = f32[2,4,128,128]{3,2,1,0:T(8,128)S(1)} collective-permute-done((f32[2,4,128,128]{3,2,1,0:T(8,128)}, f32[2,4,128,128]{3,2,1,0:T(8,128)S(1)}, u32[]{:S(2)}, u32[]{:S(2)}) %collective-permute-start) | collective-permute-done | bytes 524320 | tf_op jit(solution)/shard_map/while/body/eval_jaxpr/ppermute | solution.py:16
  144.6 11.5 %collective-permute-done = f32[2,4,128,128]{3,2,1,0:T(8,128)S(1)} collective-permute-done((f32[2,4,128,128]{3,2,1,0:T(8,128)}, f32[2,4,128,128]{3,2,1,0:T(8,128)S(1)}, u32[]{:S(2)}, u32[]{:S(2)}) %collective-permute-start) | collective-permute-done | bytes 524320 | tf_op jit(solution)/shard_map/while/body/eval_jaxpr/ppermute | solution.py:16
  159.4 1.9 collective-permute-start
  161.3 11.5 %collective-permute-done = f32[2,4,128,128]{3,2,1,0:T(8,128)S(1)} collective-permute-done((f32[2,4,128,128]{3,2,1,0:T(8,128)}, f32[2,4,128,128]{3,2,1,0:T(8,128)S(1)}, u32[]{:S(2)}, u32[]{:S(2)}) %collective-permute-start) | collective-permute-done | bytes 524320 | tf_op jit(solution)/shard_map/while/body/eval_jaxpr/ppermute | solution.py:16
  176.1 1.9 collective-permute-start
  178.0 11.5 %collective-permute-done = f32[2,4,128,128]{3,2,1,0:T(8,128)S(1)} collective-permute-done((f32[2,4,128,128]{3,2,1,0:T(8,128)}, f32[2,4,128,128]{3,2,1,0:T(8,128)S(1)}, u32[]{:S(2)}, u32[]{:S(2)}) %collective-permute-start) | collective-permute-done | bytes 524320 | tf_op jit(solution)/shard_map/while/body/eval_jaxpr/ppermute | solution.py:16
  192.9 1.9 collective-permute-start
  194.8 11.5 %collective-permute-done = f32[2,4,128,128]{3,2,1,0:T(8,128)S(1)} collective-permute-done((f32[2,4,128,128]{3,2,1,0:T(8,128)}, f32[2,4,128,128]{3,2,1,0:T(8,128)S(1)}, u32[]{:S(2)}, u32[]{:S(2)}) %collective-permute-start) | collective-permute-done | bytes 524320 | tf_op jit(solution)/shard_map/while/body/eval_jaxpr/ppermute | solution.py:16
  209.6 1.9 collective-permute-start
  211.5 11.7 %collective-permute-done = f32[2,4,128,128]{3,2,1,0:T(8,128)S(1)} collective-permute-done((f32[2,4,128,128]{3,2,1,0:T(8,128)}, f32[2,4,128,128]{3,2,1,0:T(8,128)S(1)}, u32[]{:S(2)}, u32[]{:S(2)}) %collective-permute-start) | collective-permute-done | bytes 524320 | tf_op jit(solution)/shard_map/while/body/eval_jaxpr/ppermute | solution.py:16
  226.6 1.9 collective-permute-start
  228.5 12.8 %collective-permute-done = f32[2,4,128,128]{3,2,1,0:T(8,128)S(1)} collective-permute-done((f32[2,4,128,128]{3,2,1,0:T(8,128)}, f32[2,4,128,128]{3,2,1,0:T(8,128)S(1)}, u32[]{:S(2)}, u32[]{:S(2)}) %collective-permute-start) | collective-permute-done | bytes 524320 | tf_op jit(solution)/shard_map/while/body/eval_jaxpr/ppermute | solution.py:16
  244.7 1.9 collective-permute-start
  246.6 13.9 %collective-permute-done = f32[2,4,128,128]{3,2,1,0:T(8,128)S(1)} collective-permute-done((f32[2,4,128,128]{3,2,1,0:T(8,128)}, f32[2,4,128,128]{3,2,1,0:T(8,128)S(1)}, u32[]{:S(2)}, u32[]{:S(2)}) %collective-permute-start) | collective-permute-done | bytes 524320 | tf_op jit(solution)/shard_map/while/body/eval_jaxpr/ppermute | solution.py:16
  263.8 1.9 collective-permute-start
  265.7 15.0 %collective-permute-done = f32[2,4,128,128]{3,2,1,0:T(8,128)S(1)} collective-permute-done((f32[2,4,128,128]{3,2,1,0:T(8,128)}, f32[2,4,128,128]{3,2,1,0:T(8,128)S(1)}, u32[]{:S(2)}, u32[]{:S(2)}) %collective-permute-start) | collective-permute-done | bytes 524320 | tf_op jit(solution)/shard_map/while/body/eval_jaxpr/ppermute | solution.py:16
  286.0 16.1 %collective-permute-done = f32[2,4,128,128]{3,2,1,0:T(8,128)S(1)} collective-permute-done((f32[2,4,128,128]{3,2,1,0:T(8,128)}, f32[2,4,128,128]{3,2,1,0:T(8,128)S(1)}, u32[]{:S(2)}, u32[]{:S(2)}) %collective-permute-start) | collective-permute-done | bytes 524320 | tf_op jit(solution)/shard_map/while/body/eval_jaxpr/ppermute | solution.py:16
  305.5 1.9 collective-permute-start
  307.4 16.9 %collective-permute-done = f32[2,4,128,128]{3,2,1,0:T(8,128)S(1)} collective-permute-done((f32[2,4,128,128]{3,2,1,0:T(8,128)}, f32[2,4,128,128]{3,2,1,0:T(8,128)S(1)}, u32[]{:S(2)}, u32[]{:S(2)}) %collective-permute-start) | collective-permute-done | bytes 524320 | tf_op jit(solution)/shard_map/while/body/eval_jaxpr/ppermute | solution.py:16
  329.5 41.0 %collective-permute-done = f32[2,4,128,128]{3,2,1,0:T(8,128)S(1)} collective-permute-done((f32[2,4,128,128]{3,2,1,0:T(8,128)}, f32[2,4,128,128]{3,2,1,0:T(8,128)S(1)}, u32[]{:S(2)}, u32[]{:S(2)}) %collective-permute-start) | collective-permute-done | bytes 524320 | tf_op jit(solution)/shard_map/while/body/eval_jaxpr/ppermute | solution.py:16
  373.9 1.9 collective-permute-start
  375.8 25.8 %collective-permute-done = f32[2,4,128,128]{3,2,1,0:T(8,128)S(1)} collective-permute-done((f32[2,4,128,128]{3,2,1,0:T(8,128)}, f32[2,4,128,128]{3,2,1,0:T(8,128)S(1)}, u32[]{:S(2)}, u32[]{:S(2)}) %collective-permute-start) | collective-permute-done | bytes 524320 | tf_op jit(solution)/shard_map/while/body/eval_jaxpr/ppermute | solution.py:16
  405.0 1.9 collective-permute-start
  406.9 15.7 %collective-permute-done = f32[2,4,128,128]{3,2,1,0:T(8,128)S(1)} collective-permute-done((f32[2,4,128,128]{3,2,1,0:T(8,128)}, f32[2,4,128,128]{3,2,1,0:T(8,128)S(1)}, u32[]{:S(2)}, u32[]{:S(2)}) %collective-permute-start) | collective-permute-done | bytes 524320 | tf_op jit(solution)/shard_map/while/body/eval_jaxpr/ppermute | solution.py:16
  425.9 1.9 collective-permute-start
  427.9 26.5 %collective-permute-done = f32[2,4,128,128]{3,2,1,0:T(8,128)S(1)} collective-permute-done((f32[2,4,128,128]{3,2,1,0:T(8,128)}, f32[2,4,128,128]{3,2,1,0:T(8,128)S(1)}, u32[]{:S(2)}, u32[]{:S(2)}) %collective-permute-start) | collective-permute-done | bytes 524320 | tf_op jit(solution)/shard_map/while/body/eval_jaxpr/ppermute | solution.py:16
  459.6 42.0 %collective-permute-done = f32[2,4,128,128]{3,2,1,0:T(8,128)S(1)} collective-permute-done((f32[2,4,128,128]{3,2,1,0:T(8,128)}, f32[2,4,128,128]{3,2,1,0:T(8,128)S(1)}, u32[]{:S(2)}, u32[]{:S(2)}) %collective-permute-start) | collective-permute-done | bytes 524320 | tf_op jit(solution)/shard_map/while/body/eval_jaxpr/ppermute | solution.py:16
  504.9 1.9 collective-permute-start
  506.8 21.5 %collective-permute-done = f32[2,4,128,128]{3,2,1,0:T(8,128)S(1)} collective-permute-done((f32[2,4,128,128]{3,2,1,0:T(8,128)}, f32[2,4,128,128]{3,2,1,0:T(8,128)S(1)}, u32[]{:S(2)}, u32[]{:S(2)}) %collective-permute-start) | collective-permute-done | bytes 524320 | tf_op jit(solution)/shard_map/while/body/eval_jaxpr/ppermute | solution.py:16
  531.7 1.9 collective-permute-start
  533.6 37.3 %collective-permute-done = f32[2,4,128,128]{3,2,1,0:T(8,128)S(1)} collective-permute-done((f32[2,4,128,128]{3,2,1,0:T(8,128)}, f32[2,4,128,128]{3,2,1,0:T(8,128)S(1)}, u32[]{:S(2)}, u32[]{:S(2)}) %collective-permute-start) | collective-permute-done | bytes 524320 | tf_op jit(solution)/shard_map/while/body/eval_jaxpr/ppermute | solution.py:16
  576.2 26.9 %collective-permute-done = f32[2,4,128,128]{3,2,1,0:T(8,128)S(1)} collective-permute-done((f32[2,4,128,128]{3,2,1,0:T(8,128)}, f32[2,4,128,128]{3,2,1,0:T(8,128)S(1)}, u32[]{:S(2)}, u32[]{:S(2)}) %collective-permute-start) | collective-permute-done | bytes 524320 | tf_op jit(solution)/shard_map/while/body/eval_jaxpr/ppermute | solution.py:16
  606.4 1.9 collective-permute-start
  608.3 25.9 %collective-permute-done = f32[2,4,128,128]{3,2,1,0:T(8,128)S(1)} collective-permute-done((f32[2,4,128,128]{3,2,1,0:T(8,128)}, f32[2,4,128,128]{3,2,1,0:T(8,128)S(1)}, u32[]{:S(2)}, u32[]{:S(2)}) %collective-permute-start) | collective-permute-done | bytes 524320 | tf_op jit(solution)/shard_map/while/body/eval_jaxpr/ppermute | solution.py:16
  639.5 34.8 %collective-permute-done = f32[2,4,128,128]{3,2,1,0:T(8,128)S(1)} collective-permute-done((f32[2,4,128,128]{3,2,1,0:T(8,128)}, f32[2,4,128,128]{3,2,1,0:T(8,128)S(1)}, u32[]{:S(2)}, u32[]{:S(2)}) %collective-permute-start) | collective-permute-done | bytes 524320 | tf_op jit(solution)/shard_map/while/body/eval_jaxpr/ppermute | solution.py:16
  677.7 1.9 collective-permute-start
  679.6 14.7 %collective-permute-done = f32[2,4,128,128]{3,2,1,0:T(8,128)S(1)} collective-permute-done((f32[2,4,128,128]{3,2,1,0:T(8,128)}, f32[2,4,128,128]{3,2,1,0:T(8,128)S(1)}, u32[]{:S(2)}, u32[]{:S(2)}) %collective-permute-start) | collective-permute-done | bytes 524320 | tf_op jit(solution)/shard_map/while/body/eval_jaxpr/ppermute | solution.py:16
  697.7 1.9 collective-permute-start
  699.6 15.6 %collective-permute-done = f32[2,4,128,128]{3,2,1,0:T(8,128)S(1)} collective-permute-done((f32[2,4,128,128]{3,2,1,0:T(8,128)}, f32[2,4,128,128]{3,2,1,0:T(8,128)S(1)}, u32[]{:S(2)}, u32[]{:S(2)}) %collective-permute-start) | collective-permute-done | bytes 524320 | tf_op jit(solution)/shard_map/while/body/eval_jaxpr/ppermute | solution.py:16
  718.5 1.9 collective-permute-start
  720.4 19.6 %collective-permute-done = f32[2,4,128,128]{3,2,1,0:T(8,128)S(1)} collective-permute-done((f32[2,4,128,128]{3,2,1,0:T(8,128)}, f32[2,4,128,128]{3,2,1,0:T(8,128)S(1)}, u32[]{:S(2)}, u32[]{:S(2)}) %collective-permute-start) | collective-permute-done | bytes 524320 | tf_op jit(solution)/shard_map/while/body/eval_jaxpr/ppermute | solution.py:16
  743.4 1.9 collective-permute-start
  745.3 23.4 %collective-permute-done = f32[2,4,128,128]{3,2,1,0:T(8,128)S(1)} collective-permute-done((f32[2,4,128,128]{3,2,1,0:T(8,128)}, f32[2,4,128,128]{3,2,1,0:T(8,128)S(1)}, u32[]{:S(2)}, u32[]{:S(2)}) %collective-permute-start) | collective-permute-done | bytes 524320 | tf_op jit(solution)/shard_map/while/body/eval_jaxpr/ppermute | solution.py:16
  774.0 16.0 %collective-permute-done = f32[2,4,128,128]{3,2,1,0:T(8,128)S(1)} collective-permute-done((f32[2,4,128,128]{3,2,1,0:T(8,128)}, f32[2,4,128,128]{3,2,1,0:T(8,128)S(1)}, u32[]{:S(2)}, u32[]{:S(2)}) %collective-permute-start) | collective-permute-done | bytes 524320 | tf_op jit(solution)/shard_map/while/body/eval_jaxpr/ppermute | solution.py:16
  795.3 16.4 %collective-permute-done = f32[2,4,128,128]{3,2,1,0:T(8,128)S(1)} collective-permute-done((f32[2,4,128,128]{3,2,1,0:T(8,128)}, f32[2,4,128,128]{3,2,1,0:T(8,128)S(1)}, u32[]{:S(2)}, u32[]{:S(2)}) %collective-permute-start) | collective-permute-done | bytes 524320 | tf_op jit(solution)/shard_map/while/body/eval_jaxpr/ppermute | solution.py:16
  813.5 23.8 %while.40 = (s32[]{:T(128)}, f32[2,4,128,128]{3,2,1,0:T(8,128)S(1)}, f32[4,2,4,64,128]{4,3,2,1,0:T(8,128)}, f32[4,2,4,64,128]{4,3,2,1,0:T(8,128)S(1)}, f32[4,2,4...) while((s32[]{:T(128)}, ...), condition=%wide.region_5.7_spmd.clone, body=%wide.region_4.6_spmd.clone.sunk | while | flops 403050496 | bytes 6055025 | solution.py:73
  841.1 7.8 fusion.36
  848.9 250.4 %reduce-scatter.2.cloned.1.call-done = f32[32,2,4096]{2,0,1:T(8,128)} async-done(((f32[256,2,4096]{2,0,1:T(8,128)}), f32[32,2,4096]{2,0,1:T(8,128)}) %reduce-scatter.2.cloned.1.call-update) | async-done | bytes 1048592 | tf_op jit(solution)/shard_map/reduce_scatter | solution.py:82
  (223 shorter events, 172.6 us)
Async XLA Ops:
  6.5 3.5 copy-start
  6.5 1092.8 %reduce-scatter.2.cloned.1.call-start = ((), (), s32[]{:S(2)}) async-start(), calls=%async_computation.1 | async-start | bytes 9437184 | tf_op jit(solution)/shard_map/reduce_scatter | solution.py:82
  25.8 18.4 %copy-start.2 = (f32[4,128,128]{2,1,0:T(8,128)S(1)}, f32[4,128,128]{2,1,0:T(8,128)}, u32[]{:S(2)}) copy-start(f32[4,128,128]{2,1,0:T(8,128)} %param.22) | copy-start | bytes 786436
  45.7 17.9 %collective-permute-start = (f32[2,4,128,128]{3,2,1,0:T(8,128)}, f32[2,4,128,128]{3,2,1,0:T(8,128)S(1)}, u32[]{:S(2)}, u32[]{:S(2)}) collective-permute-start(f32[2,4,128,128]{3,2,1,0:T(8,128)} %convolution_add_fusion.4), channel_id=1, source_target_pairs={{0,8},{8,16},{16,24},{24,32},{32,40},{40,48},{48,56},{56,64},{64,7... | collective-permute-start | bytes 1572872 | tf_op jit(solution)/shard_map/while/body/eval_jaxpr/ppermute | solution.py:16
  63.5 0.8 copy-start.1
  66.9 17.0 %collective-permute-start = (f32[2,4,128,128]{3,2,1,0:T(8,128)}, f32[2,4,128,128]{3,2,1,0:T(8,128)S(1)}, u32[]{:S(2)}, u32[]{:S(2)}) collective-permute-start(f32[2,4,128,128]{3,2,1,0:T(8,128)} %convolution_add_fusion.4), channel_id=1, source_target_pairs={{0,8},{8,16},{16,24},{24,32},{32,40},{40,48},{48,56},{56,64},{64,7... | collective-permute-start | bytes 1572872 | tf_op jit(solution)/shard_map/while/body/eval_jaxpr/ppermute | solution.py:16
  83.9 0.8 copy-start.1
  87.2 16.1 %collective-permute-start = (f32[2,4,128,128]{3,2,1,0:T(8,128)}, f32[2,4,128,128]{3,2,1,0:T(8,128)S(1)}, u32[]{:S(2)}, u32[]{:S(2)}) collective-permute-start(f32[2,4,128,128]{3,2,1,0:T(8,128)} %convolution_add_fusion.4), channel_id=1, source_target_pairs={{0,8},{8,16},{16,24},{24,32},{32,40},{40,48},{48,56},{56,64},{64,7... | collective-permute-start | bytes 1572872 | tf_op jit(solution)/shard_map/while/body/eval_jaxpr/ppermute | solution.py:16
  103.3 0.8 copy-start.1
  106.6 15.1 %collective-permute-start = (f32[2,4,128,128]{3,2,1,0:T(8,128)}, f32[2,4,128,128]{3,2,1,0:T(8,128)S(1)}, u32[]{:S(2)}, u32[]{:S(2)}) collective-permute-start(f32[2,4,128,128]{3,2,1,0:T(8,128)} %convolution_add_fusion.4), channel_id=1, source_target_pairs={{0,8},{8,16},{16,24},{24,32},{32,40},{40,48},{48,56},{56,64},{64,7... | collective-permute-start | bytes 1572872 | tf_op jit(solution)/shard_map/while/body/eval_jaxpr/ppermute | solution.py:16
  121.8 0.8 copy-start.1
  125.1 14.2 %collective-permute-start = (f32[2,4,128,128]{3,2,1,0:T(8,128)}, f32[2,4,128,128]{3,2,1,0:T(8,128)S(1)}, u32[]{:S(2)}, u32[]{:S(2)}) collective-permute-start(f32[2,4,128,128]{3,2,1,0:T(8,128)} %convolution_add_fusion.4), channel_id=1, source_target_pairs={{0,8},{8,16},{16,24},{24,32},{32,40},{40,48},{48,56},{56,64},{64,7... | collective-permute-start | bytes 1572872 | tf_op jit(solution)/shard_map/while/body/eval_jaxpr/ppermute | solution.py:16
  139.3 0.8 copy-start.1
  142.7 13.4 %collective-permute-start = (f32[2,4,128,128]{3,2,1,0:T(8,128)}, f32[2,4,128,128]{3,2,1,0:T(8,128)S(1)}, u32[]{:S(2)}, u32[]{:S(2)}) collective-permute-start(f32[2,4,128,128]{3,2,1,0:T(8,128)} %convolution_add_fusion.4), channel_id=1, source_target_pairs={{0,8},{8,16},{16,24},{24,32},{32,40},{40,48},{48,56},{56,64},{64,7... | collective-permute-start | bytes 1572872 | tf_op jit(solution)/shard_map/while/body/eval_jaxpr/ppermute | solution.py:16
  156.1 0.8 copy-start.1
  159.4 13.4 %collective-permute-start = (f32[2,4,128,128]{3,2,1,0:T(8,128)}, f32[2,4,128,128]{3,2,1,0:T(8,128)S(1)}, u32[]{:S(2)}, u32[]{:S(2)}) collective-permute-start(f32[2,4,128,128]{3,2,1,0:T(8,128)} %convolution_add_fusion.4), channel_id=1, source_target_pairs={{0,8},{8,16},{16,24},{24,32},{32,40},{40,48},{48,56},{56,64},{64,7... | collective-permute-start | bytes 1572872 | tf_op jit(solution)/shard_map/while/body/eval_jaxpr/ppermute | solution.py:16
  172.8 0.8 copy-start.1
  176.1 13.4 %collective-permute-start = (f32[2,4,128,128]{3,2,1,0:T(8,128)}, f32[2,4,128,128]{3,2,1,0:T(8,128)S(1)}, u32[]{:S(2)}, u32[]{:S(2)}) collective-permute-start(f32[2,4,128,128]{3,2,1,0:T(8,128)} %convolution_add_fusion.4), channel_id=1, source_target_pairs={{0,8},{8,16},{16,24},{24,32},{32,40},{40,48},{48,56},{56,64},{64,7... | collective-permute-start | bytes 1572872 | tf_op jit(solution)/shard_map/while/body/eval_jaxpr/ppermute | solution.py:16
  189.5 0.8 copy-start.1
  192.9 13.4 %collective-permute-start = (f32[2,4,128,128]{3,2,1,0:T(8,128)}, f32[2,4,128,128]{3,2,1,0:T(8,128)S(1)}, u32[]{:S(2)}, u32[]{:S(2)}) collective-permute-start(f32[2,4,128,128]{3,2,1,0:T(8,128)} %convolution_add_fusion.4), channel_id=1, source_target_pairs={{0,8},{8,16},{16,24},{24,32},{32,40},{40,48},{48,56},{56,64},{64,7... | collective-permute-start | bytes 1572872 | tf_op jit(solution)/shard_map/while/body/eval_jaxpr/ppermute | solution.py:16
  206.2 0.8 copy-start.1
  209.6 13.7 %collective-permute-start = (f32[2,4,128,128]{3,2,1,0:T(8,128)}, f32[2,4,128,128]{3,2,1,0:T(8,128)S(1)}, u32[]{:S(2)}, u32[]{:S(2)}) collective-permute-start(f32[2,4,128,128]{3,2,1,0:T(8,128)} %convolution_add_fusion.4), channel_id=1, source_target_pairs={{0,8},{8,16},{16,24},{24,32},{32,40},{40,48},{48,56},{56,64},{64,7... | collective-permute-start | bytes 1572872 | tf_op jit(solution)/shard_map/while/body/eval_jaxpr/ppermute | solution.py:16
  223.2 0.8 copy-start.1
  226.6 14.7 %collective-permute-start = (f32[2,4,128,128]{3,2,1,0:T(8,128)}, f32[2,4,128,128]{3,2,1,0:T(8,128)S(1)}, u32[]{:S(2)}, u32[]{:S(2)}) collective-permute-start(f32[2,4,128,128]{3,2,1,0:T(8,128)} %convolution_add_fusion.4), channel_id=1, source_target_pairs={{0,8},{8,16},{16,24},{24,32},{32,40},{40,48},{48,56},{56,64},{64,7... | collective-permute-start | bytes 1572872 | tf_op jit(solution)/shard_map/while/body/eval_jaxpr/ppermute | solution.py:16
  241.3 0.8 copy-start.1
  244.7 15.8 %collective-permute-start = (f32[2,4,128,128]{3,2,1,0:T(8,128)}, f32[2,4,128,128]{3,2,1,0:T(8,128)S(1)}, u32[]{:S(2)}, u32[]{:S(2)}) collective-permute-start(f32[2,4,128,128]{3,2,1,0:T(8,128)} %convolution_add_fusion.4), channel_id=1, source_target_pairs={{0,8},{8,16},{16,24},{24,32},{32,40},{40,48},{48,56},{56,64},{64,7... | collective-permute-start | bytes 1572872 | tf_op jit(solution)/shard_map/while/body/eval_jaxpr/ppermute | solution.py:16
  260.5 0.8 copy-start.1
  263.8 16.9 %collective-permute-start = (f32[2,4,128,128]{3,2,1,0:T(8,128)}, f32[2,4,128,128]{3,2,1,0:T(8,128)S(1)}, u32[]{:S(2)}, u32[]{:S(2)}) collective-permute-start(f32[2,4,128,128]{3,2,1,0:T(8,128)} %convolution_add_fusion.4), channel_id=1, source_target_pairs={{0,8},{8,16},{16,24},{24,32},{32,40},{40,48},{48,56},{56,64},{64,7... | collective-permute-start | bytes 1572872 | tf_op jit(solution)/shard_map/while/body/eval_jaxpr/ppermute | solution.py:16
  280.7 0.8 copy-start.1
  284.1 18.1 %collective-permute-start = (f32[2,4,128,128]{3,2,1,0:T(8,128)}, f32[2,4,128,128]{3,2,1,0:T(8,128)S(1)}, u32[]{:S(2)}, u32[]{:S(2)}) collective-permute-start(f32[2,4,128,128]{3,2,1,0:T(8,128)} %convolution_add_fusion.4), channel_id=1, source_target_pairs={{0,8},{8,16},{16,24},{24,32},{32,40},{40,48},{48,56},{56,64},{64,7... | collective-permute-start | bytes 1572872 | tf_op jit(solution)/shard_map/while/body/eval_jaxpr/ppermute | solution.py:16
  302.1 0.8 copy-start.1
  305.5 18.8 %collective-permute-start = (f32[2,4,128,128]{3,2,1,0:T(8,128)}, f32[2,4,128,128]{3,2,1,0:T(8,128)S(1)}, u32[]{:S(2)}, u32[]{:S(2)}) collective-permute-start(f32[2,4,128,128]{3,2,1,0:T(8,128)} %convolution_add_fusion.4), channel_id=1, source_target_pairs={{0,8},{8,16},{16,24},{24,32},{32,40},{40,48},{48,56},{56,64},{64,7... | collective-permute-start | bytes 1572872 | tf_op jit(solution)/shard_map/while/body/eval_jaxpr/ppermute | solution.py:16
  324.3 0.8 copy-start.1
  327.6 43.0 %collective-permute-start = (f32[2,4,128,128]{3,2,1,0:T(8,128)}, f32[2,4,128,128]{3,2,1,0:T(8,128)S(1)}, u32[]{:S(2)}, u32[]{:S(2)}) collective-permute-start(f32[2,4,128,128]{3,2,1,0:T(8,128)} %convolution_add_fusion.4), channel_id=1, source_target_pairs={{0,8},{8,16},{16,24},{24,32},{32,40},{40,48},{48,56},{56,64},{64,7... | collective-permute-start | bytes 1572872 | tf_op jit(solution)/shard_map/while/body/eval_jaxpr/ppermute | solution.py:16
  370.6 0.8 copy-start.1
  373.9 27.7 %collective-permute-start = (f32[2,4,128,128]{3,2,1,0:T(8,128)}, f32[2,4,128,128]{3,2,1,0:T(8,128)S(1)}, u32[]{:S(2)}, u32[]{:S(2)}) collective-permute-start(f32[2,4,128,128]{3,2,1,0:T(8,128)} %convolution_add_fusion.4), channel_id=1, source_target_pairs={{0,8},{8,16},{16,24},{24,32},{32,40},{40,48},{48,56},{56,64},{64,7... | collective-permute-start | bytes 1572872 | tf_op jit(solution)/shard_map/while/body/eval_jaxpr/ppermute | solution.py:16
  401.6 0.8 copy-start.1
  405.0 17.6 %collective-permute-start = (f32[2,4,128,128]{3,2,1,0:T(8,128)}, f32[2,4,128,128]{3,2,1,0:T(8,128)S(1)}, u32[]{:S(2)}, u32[]{:S(2)}) collective-permute-start(f32[2,4,128,128]{3,2,1,0:T(8,128)} %convolution_add_fusion.4), channel_id=1, source_target_pairs={{0,8},{8,16},{16,24},{24,32},{32,40},{40,48},{48,56},{56,64},{64,7... | collective-permute-start | bytes 1572872 | tf_op jit(solution)/shard_map/while/body/eval_jaxpr/ppermute | solution.py:16
  422.6 0.8 copy-start.1
  425.9 28.4 %collective-permute-start = (f32[2,4,128,128]{3,2,1,0:T(8,128)}, f32[2,4,128,128]{3,2,1,0:T(8,128)S(1)}, u32[]{:S(2)}, u32[]{:S(2)}) collective-permute-start(f32[2,4,128,128]{3,2,1,0:T(8,128)} %convolution_add_fusion.4), channel_id=1, source_target_pairs={{0,8},{8,16},{16,24},{24,32},{32,40},{40,48},{48,56},{56,64},{64,7... | collective-permute-start | bytes 1572872 | tf_op jit(solution)/shard_map/while/body/eval_jaxpr/ppermute | solution.py:16
  454.3 0.8 copy-start.1
  457.7 43.9 %collective-permute-start = (f32[2,4,128,128]{3,2,1,0:T(8,128)}, f32[2,4,128,128]{3,2,1,0:T(8,128)S(1)}, u32[]{:S(2)}, u32[]{:S(2)}) collective-permute-start(f32[2,4,128,128]{3,2,1,0:T(8,128)} %convolution_add_fusion.4), channel_id=1, source_target_pairs={{0,8},{8,16},{16,24},{24,32},{32,40},{40,48},{48,56},{56,64},{64,7... | collective-permute-start | bytes 1572872 | tf_op jit(solution)/shard_map/while/body/eval_jaxpr/ppermute | solution.py:16
  501.5 0.8 copy-start.1
  504.9 23.4 %collective-permute-start = (f32[2,4,128,128]{3,2,1,0:T(8,128)}, f32[2,4,128,128]{3,2,1,0:T(8,128)S(1)}, u32[]{:S(2)}, u32[]{:S(2)}) collective-permute-start(f32[2,4,128,128]{3,2,1,0:T(8,128)} %convolution_add_fusion.4), channel_id=1, source_target_pairs={{0,8},{8,16},{16,24},{24,32},{32,40},{40,48},{48,56},{56,64},{64,7... | collective-permute-start | bytes 1572872 | tf_op jit(solution)/shard_map/while/body/eval_jaxpr/ppermute | solution.py:16
  528.3 0.8 copy-start.1
  531.7 39.2 %collective-permute-start = (f32[2,4,128,128]{3,2,1,0:T(8,128)}, f32[2,4,128,128]{3,2,1,0:T(8,128)S(1)}, u32[]{:S(2)}, u32[]{:S(2)}) collective-permute-start(f32[2,4,128,128]{3,2,1,0:T(8,128)} %convolution_add_fusion.4), channel_id=1, source_target_pairs={{0,8},{8,16},{16,24},{24,32},{32,40},{40,48},{48,56},{56,64},{64,7... | collective-permute-start | bytes 1572872 | tf_op jit(solution)/shard_map/while/body/eval_jaxpr/ppermute | solution.py:16
  570.9 0.8 copy-start.1
  574.2 28.8 %collective-permute-start = (f32[2,4,128,128]{3,2,1,0:T(8,128)}, f32[2,4,128,128]{3,2,1,0:T(8,128)S(1)}, u32[]{:S(2)}, u32[]{:S(2)}) collective-permute-start(f32[2,4,128,128]{3,2,1,0:T(8,128)} %convolution_add_fusion.4), channel_id=1, source_target_pairs={{0,8},{8,16},{16,24},{24,32},{32,40},{40,48},{48,56},{56,64},{64,7... | collective-permute-start | bytes 1572872 | tf_op jit(solution)/shard_map/while/body/eval_jaxpr/ppermute | solution.py:16
  603.1 0.8 copy-start.1
  606.4 27.9 %collective-permute-start = (f32[2,4,128,128]{3,2,1,0:T(8,128)}, f32[2,4,128,128]{3,2,1,0:T(8,128)S(1)}, u32[]{:S(2)}, u32[]{:S(2)}) collective-permute-start(f32[2,4,128,128]{3,2,1,0:T(8,128)} %convolution_add_fusion.4), channel_id=1, source_target_pairs={{0,8},{8,16},{16,24},{24,32},{32,40},{40,48},{48,56},{56,64},{64,7... | collective-permute-start | bytes 1572872 | tf_op jit(solution)/shard_map/while/body/eval_jaxpr/ppermute | solution.py:16
  637.6 36.7 %collective-permute-start = (f32[2,4,128,128]{3,2,1,0:T(8,128)}, f32[2,4,128,128]{3,2,1,0:T(8,128)S(1)}, u32[]{:S(2)}, u32[]{:S(2)}) collective-permute-start(f32[2,4,128,128]{3,2,1,0:T(8,128)} %convolution_add_fusion.4), channel_id=1, source_target_pairs={{0,8},{8,16},{16,24},{24,32},{32,40},{40,48},{48,56},{56,64},{64,7... | collective-permute-start | bytes 1572872 | tf_op jit(solution)/shard_map/while/body/eval_jaxpr/ppermute | solution.py:16
  674.3 0.8 copy-start.1
  677.7 16.7 %collective-permute-start = (f32[2,4,128,128]{3,2,1,0:T(8,128)}, f32[2,4,128,128]{3,2,1,0:T(8,128)S(1)}, u32[]{:S(2)}, u32[]{:S(2)}) collective-permute-start(f32[2,4,128,128]{3,2,1,0:T(8,128)} %convolution_add_fusion.4), channel_id=1, source_target_pairs={{0,8},{8,16},{16,24},{24,32},{32,40},{40,48},{48,56},{56,64},{64,7... | collective-permute-start | bytes 1572872 | tf_op jit(solution)/shard_map/while/body/eval_jaxpr/ppermute | solution.py:16
  694.3 0.8 copy-start.1
  697.7 17.5 %collective-permute-start = (f32[2,4,128,128]{3,2,1,0:T(8,128)}, f32[2,4,128,128]{3,2,1,0:T(8,128)S(1)}, u32[]{:S(2)}, u32[]{:S(2)}) collective-permute-start(f32[2,4,128,128]{3,2,1,0:T(8,128)} %convolution_add_fusion.4), channel_id=1, source_target_pairs={{0,8},{8,16},{16,24},{24,32},{32,40},{40,48},{48,56},{56,64},{64,7... | collective-permute-start | bytes 1572872 | tf_op jit(solution)/shard_map/while/body/eval_jaxpr/ppermute | solution.py:16
  715.1 0.8 copy-start.1
  718.5 21.5 %collective-permute-start = (f32[2,4,128,128]{3,2,1,0:T(8,128)}, f32[2,4,128,128]{3,2,1,0:T(8,128)S(1)}, u32[]{:S(2)}, u32[]{:S(2)}) collective-permute-start(f32[2,4,128,128]{3,2,1,0:T(8,128)} %convolution_add_fusion.4), channel_id=1, source_target_pairs={{0,8},{8,16},{16,24},{24,32},{32,40},{40,48},{48,56},{56,64},{64,7... | collective-permute-start | bytes 1572872 | tf_op jit(solution)/shard_map/while/body/eval_jaxpr/ppermute | solution.py:16
  740.0 0.8 copy-start.1
  743.4 25.4 %collective-permute-start = (f32[2,4,128,128]{3,2,1,0:T(8,128)}, f32[2,4,128,128]{3,2,1,0:T(8,128)S(1)}, u32[]{:S(2)}, u32[]{:S(2)}) collective-permute-start(f32[2,4,128,128]{3,2,1,0:T(8,128)} %convolution_add_fusion.4), channel_id=1, source_target_pairs={{0,8},{8,16},{16,24},{24,32},{32,40},{40,48},{48,56},{56,64},{64,7... | collective-permute-start | bytes 1572872 | tf_op jit(solution)/shard_map/while/body/eval_jaxpr/ppermute | solution.py:16
  772.1 17.9 %collective-permute-start = (f32[2,4,128,128]{3,2,1,0:T(8,128)}, f32[2,4,128,128]{3,2,1,0:T(8,128)S(1)}, u32[]{:S(2)}, u32[]{:S(2)}) collective-permute-start(f32[2,4,128,128]{3,2,1,0:T(8,128)} %convolution_add_fusion.4), channel_id=1, source_target_pairs={{0,8},{8,16},{16,24},{24,32},{32,40},{40,48},{48,56},{56,64},{64,7... | collective-permute-start | bytes 1572872 | tf_op jit(solution)/shard_map/while/body/eval_jaxpr/ppermute | solution.py:16
  790.0 0.8 copy-start.1
  793.3 18.3 %collective-permute-start = (f32[2,4,128,128]{3,2,1,0:T(8,128)}, f32[2,4,128,128]{3,2,1,0:T(8,128)S(1)}, u32[]{:S(2)}, u32[]{:S(2)}) collective-permute-start(f32[2,4,128,128]{3,2,1,0:T(8,128)} %convolution_add_fusion.4), channel_id=1, source_target_pairs={{0,8},{8,16},{16,24},{24,32},{32,40},{40,48},{48,56},{56,64},{64,7... | collective-permute-start | bytes 1572872 | tf_op jit(solution)/shard_map/while/body/eval_jaxpr/ppermute | solution.py:16
  811.6 0.8 copy-start.1
  813.5 25.4 %copy-start.3 = (f32[512]{0:T(512)S(1)}, f32[512]{0:T(512)}, u32[]{:S(2)}) copy-start(f32[512]{0:T(512)} %param.23) | copy-start | bytes 6148
  (2 other events, 1.6 us)
Sparse Core Ops, SparseCore 0:
  849.0 250.2 reduce-scatter.1
where the time goes:
time: 1120 us; the launch traced here: 1110 us
  waiting for transfers between devices  855 us (76%)
  matrix products  89.9 us (8%)
  starting transfers between devices  60.7 us (5%)
  local copies, waits for them, and re-layouts  45.2 us (4%)
  other arithmetic  43 us (4%)
  between operations  13.6 us (1%)
    ppermute x31, waiting for transfers between devices, passed_along(): return lax.ppermute(block, axis, route)  605 us
    reduce_scatter x1, waiting for transfers between devices, per_device(): lax.psum_scatter(product.reshape(count, seqs, out_proj.shape[1]), 'head',...  250 us
    ppermute x31, starting transfers between devices, passed_along(): return lax.ppermute(block, axis, route)  60.7 us
    dot_general x39, matrix products, matmul_state(): jnp.einsum('shij,shjk->shik', left, right, precision=lax.Precision.HIGHEST)  49.9 us
    select_n x31, other arithmetic, turn(): return jnp.where(position == 0, start, moved)  33.7 us
    while x70, local copies, waits for them, and re-layouts  24.9 us
  transfers between devices with their start and end apart: 32, of which 32 were waited for; matrix products, arithmetic and copies ran while one was open for 0% of the time, Pallas kernels for 0%

commit v1 on v0

v1 whole, which is shorter than its diff:
```python
import jax
import jax.numpy as jnp
from jax import lax
from jax.experimental import pallas as pl
from jax.experimental.pallas import tpu as pltpu
from jax.sharding import PartitionSpec as P

HS = 128
MB = 64
EPS = 1e-06
MESH = pl.DeviceIdType.MESH
F32 = jnp.float32
BF16 = jnp.bfloat16
PLANE = 16
SLOTS = 4


def halves(a):
    hi = a.astype(BF16)
    return hi, (a - hi.astype(F32)).astype(BF16)


def mm(a, b):
    return jnp.dot(a, b, preferred_element_type=F32)


def mm3(a, b):
    return mm(a[0], b[0]) + (mm(a[0], b[1]) + mm(a[1], b[0]))


def nt(a, b):
    return lax.dot_general(a, b, (((1,), (1,)), ((), ())), preferred_element_type=F32)


def tn(a, b):
    return lax.dot_general(a, b, (((0,), (0,)), ((), ())), preferred_element_type=F32)


def slice_maps(q, k, v, ecol):
    rows = k.shape[0]
    gram = nt(k, k)
    kv = jnp.concatenate([k, v], axis=1).astype(F32)
    first = halves(kv[:MB] * ecol[:MB])
    his, los = [first[0]], [first[1]]
    for start in range(MB, rows, MB):
        left = halves(gram[start : start + MB, :start])
        hi, lo = jnp.concatenate(his, axis=0), jnp.concatenate(los, axis=0)
        part = kv[start : start + MB] - mm3(left, (hi, lo))
        nxt = halves(part * ecol[start : start + MB])
        his.append(nxt[0])
        los.append(nxt[1])
    hi, lo = jnp.concatenate(his, axis=0), jnp.concatenate(los, axis=0)
    moved = tn(k, hi) + tn(k, lo)
    r = lax.broadcasted_iota(jnp.int32, (HS, HS), 0)
    c = lax.broadcasted_iota(jnp.int32, (HS, HS), 1)
    eye = jnp.where(r == c, 1.0, 0.0).astype(F32)
    fd = jnp.concatenate([eye - moved[:, :HS], moved[:, HS:]], axis=1)
    scores = nt(q, k)
    r = lax.broadcasted_iota(jnp.int32, (rows, rows), 0)
    c = lax.broadcasted_iota(jnp.int32, (rows, rows), 1)
    scores = halves(jnp.where(c <= r, scores, 0.0))
    read = mm3(scores, (hi, lo))
    return fd, q.astype(F32) - read[:, :HS], read[:, HS:]


def local_kernel(q_ref, k_ref, v_ref, gate_ref, rate_ref, fd_ref, qh_ref, ql_ref, z0_ref):
    heads = gate_ref.shape[1]
    rows = gate_ref.shape[2]
    gate = gate_ref[0]
    eta = jnp.concatenate(
        [gate[h : h + 1] * rate_ref[h] for h in range(heads)] + [jnp.zeros((8 - heads, rows), F32)], axis=0
    )
    etat = eta.T
    for h in range(heads):
        cols = slice(h * HS, (h + 1) * HS)
        fd, qt, z0 = slice_maps(q_ref[0, :, cols], k_ref[0, :, cols], v_ref[0, :, cols], etat[:, h : h + 1])
        fd_ref[h] = fd
        hi, lo = halves(qt)
        qh_ref[h] = hi
        ql_ref[h] = lo
        z0_ref[h] = z0


def copy_wait(ref, sem):
    pltpu.make_async_copy(ref, ref, sem).wait()


def scan_kernel(
    fd_ref, init_ref, w_ref, recv, hist, wout, xw, wbuf, fd_send, fd_recv, w_send, w_recv, x_send, x_recv
):
    me_c, me_h = lax.axis_index("ctx"), lax.axis_index("head")
    zhi, p = me_c // PLANE, lax.rem(me_c, PLANE)
    x, y = p // 4, lax.rem(p, 4)
    core = lax.rem(me_h, 2)
    pairs = fd_ref.shape[0]
    heads = init_ref.shape[0]

    barrier = pltpu.get_barrier_semaphore()
    for step in range(1, PLANE):
        other = zhi * PLANE + lax.rem(p + step, PLANE)
        pl.semaphore_signal(barrier, inc=1, device_id=(other, me_h), device_id_type=MESH)
    partner = (1 - zhi) * PLANE + p
    pl.semaphore_signal(barrier, inc=1, device_id=(partner, me_h), device_id_type=MESH)
    pl.semaphore_wait(barrier, PLANE)

    def home(j):
        s, hh = j // heads, j % heads
        return 4 * hh + 2 * core + (hh + s) % 2

    def fd_copy(j):
        return pltpu.make_async_remote_copy(
            src_ref=fd_ref.at[j],
            dst_ref=recv.at[p],
            send_sem=fd_send.at[j],
            recv_sem=fd_recv.at[p],
            device_id=(zhi * PLANE + home(j), me_h),
            device_id_type=MESH,
        )

    for j in range(pairs):
        to = home(j)

        @pl.when(to != p)
        def _():
            fd_copy(j).start()

        @pl.when(to == p)
        def _():
            pltpu.make_async_copy(fd_ref.at[j], recv.at[p], fd_recv.at[p]).start()

    handler = y // 2 == core
    mine = lax.rem(x + y, 2) * heads + x

    def w_copy(c):
        return pltpu.make_async_remote_copy(
            src_ref=wout.at[c],
            dst_ref=wbuf.at[mine],
            send_sem=w_send.at[c],
            recv_sem=w_recv.at[mine],
            device_id=(zhi * PLANE + c, me_h),
            device_id_type=MESH,
        )

    def give(c):
        @pl.when(c != p)
        def _():
            w_copy(c).start()

        @pl.when(c == p)
        def _():
            pltpu.make_async_copy(wout.at[c], wbuf.at[mine], w_recv.at[mine]).start()

    x_copy = pltpu.make_async_remote_copy(
        src_ref=xw.at[0],
        dst_ref=xw.at[1],
        send_sem=x_send,
        recv_sem=x_recv,
        device_id=(PLANE + p, me_h),
        device_id_type=MESH,
    )

    @pl.when(handler)
    def _():
        r = lax.broadcasted_iota(jnp.int32, (HS, HS), 0)
        c = lax.broadcasted_iota(jnp.int32, (HS, HS), 1)
        eye = jnp.where(r == c, 1.0, 0.0).astype(F32)
        first = jnp.where(zhi == 0, 1.0, 0.0).astype(F32)
        start = jnp.concatenate([eye * (1.0 - first), init_ref[x] * first], axis=1)

        def step(c, state):
            copy_wait(recv.at[c], fd_recv.at[c])

            @pl.when(zhi == 0)
            def _():
                wout[c] = state[:, HS:]
                give(c)

            @pl.when(zhi == 1)
            def _():
                hist[c] = state

            fd = recv[c]
            nxt = mm3(halves(fd[:, :HS]), halves(state))
            return nxt + jnp.concatenate([jnp.zeros((HS, HS), F32), fd[:, HS:]], axis=1)

        last = lax.fori_loop(0, PLANE, step, start)

        @pl.when(zhi == 0)
        def _():
            xw[0] = last[:, HS:]
            x_copy.start()

        @pl.when(zhi == 1)
        def _():
            x_copy.wait_recv()
            entry = halves(xw[1])

            def apply(c, carry):
                state = hist[c]
                wout[c] = mm3(halves(state[:, :HS]), entry) + state[:, HS:]
                give(c)
                return carry

            lax.fori_loop(0, PLANE, apply, 0)

    for j in range(pairs):
        copy_wait(wbuf.at[j], w_recv.at[j])
        w_ref[j] = wbuf[j]

    for j in range(pairs):

        @pl.when(home(j) != p)
        def _():
            fd_copy(j).wait_send()

    @pl.when(handler)
    def _():
        def done(c, carry):
            @pl.when(c != p)
            def _():
                w_copy(c).wait_send()

            return carry

        lax.fori_loop(0, PLANE, done, 0)

        @pl.when(zhi == 0)
        def _():
            x_copy.wait_send()


def out_kernel(
    qh_ref, ql_ref, z0_ref, w_ref, gain_ref, proj_ref, out_ref,
    normed, prod, sib, rbuf, lbuf, sib_send, sib_recv, r_send, r_recv, l_send, l_recv,
):
    me_c, me_h = lax.axis_index("ctx"), lax.axis_index("head")
    z, core = me_h // 2, lax.rem(me_h, 2)
    twin = z * 2 + (1 - core)
    seqs, parts = prod.shape[0], prod.shape[1]
    width = prod.shape[-1]
    heads = qh_ref.shape[0] // seqs
    rows = qh_ref.shape[1]

    barrier = pltpu.get_barrier_semaphore()
    pl.semaphore_signal(barrier, inc=1, device_id=(me_c, twin), device_id_type=MESH)

    @pl.when(z > 0)
    def _():
        pl.semaphore_signal(barrier, inc=1, device_id=(me_c, me_h - 2), device_id_type=MESH)

    @pl.when(z < SLOTS - 1)
    def _():
        pl.semaphore_signal(barrier, inc=1, device_id=(me_c, me_h + 2), device_id_type=MESH)

    count = 1 + jnp.where(z > 0, 1, 0) + jnp.where(z < SLOTS - 1, 1, 0)
    pl.semaphore_wait(barrier, count)

    def sib_copy(s, q):
        return pltpu.make_async_remote_copy(
            src_ref=prod.at[s, q, 1 - core],
            dst_ref=sib.at[s, q],
            send_sem=sib_send.at[s, q],
            recv_sem=sib_recv.at[s, q],
            device_id=(me_c, twin),
            device_id_type=MESH,
        )

    def line_copy(s, q, b, step):
        buf, send, recv = (rbuf, r_send, r_recv) if step > 0 else (lbuf, l_send, l_recv)
        return pltpu.make_async_remote_copy(
            src_ref=prod.at[s, q, core, b],
            dst_ref=buf.at[s, q, b],
            send_sem=send.at[s, q, b],
            recv_sem=recv.at[s, q, b],
            device_id=(me_c, me_h + step),
            device_id_type=MESH,
        )

    for s in range(seqs):
        for h in range(heads):
            j = s * heads + h
            cols = slice(h * HS, (h + 1) * HS)
            zval = mm3((qh_ref[j], ql_ref[j]), halves(w_ref[j])) + z0_ref[j]
            scale = lax.rsqrt(jnp.mean(zval * zval, axis=-1, keepdims=True) + EPS)
            normed[s, :, cols] = (zval * scale * gain_ref[:, cols]).astype(BF16)

        def project(q, carry):
            start = pl.multiple_of(q * width, width)
            part = mm(normed[s], proj_ref[:, pl.ds(start, width)])
            part = part.reshape(SLOTS, 2, rows // (2 * SLOTS), width)
            prod[s, q, 0] = part[:, 0]
            prod[s, q, 1] = part[:, 1]
            sib_copy(s, q).start()
            return carry

        lax.fori_loop(0, parts, project, 0)

    def each(body):
        lax.fori_loop(0, seqs * parts, lambda i, carry: (body(i // parts, lax.rem(i, parts)), carry)[1], 0)

    def pair_sum(s, q):
        sib_copy(s, q).wait_recv()
        sib_copy(s, q).wait_send()
        for b in range(SLOTS):
            prod[s, q, core, b] += sib[s, q, b]

        @pl.when(z == 0)
        def _():
            for b in range(SLOTS - 1, 0, -1):
                line_copy(s, q, b, 2).start()

        @pl.when(z == SLOTS - 1)
        def _():
            for b in range(SLOTS - 1):
                line_copy(s, q, b, -2).start()

    each(pair_sum)

    def forward(s, q):
        for b in range(SLOTS - 1, 0, -1):

            @pl.when(jnp.logical_and(z > 0, z < b))
            def _():
                copy_wait(rbuf.at[s, q, b], r_recv.at[s, q, b])
                prod[s, q, core, b] += rbuf[s, q, b]
                line_copy(s, q, b, 2).start()

        for b in range(SLOTS - 1):

            @pl.when(jnp.logical_and(z < SLOTS - 1, z > b))
            def _():
                copy_wait(lbuf.at[s, q, b], l_recv.at[s, q, b])
                prod[s, q, core, b] += lbuf[s, q, b]
                line_copy(s, q, b, -2).start()

    @pl.when(jnp.logical_and(z > 0, z < SLOTS - 1))
    def _():
        each(forward)

    for s in range(seqs):
        for q in range(parts):
            cols = slice(q * width, (q + 1) * width)

            @pl.when(z > 0)
            def _():
                copy_wait(rbuf.at[s, q, z], r_recv.at[s, q, z])
                prod[s, q, core, z] += rbuf[s, q, z]

            @pl.when(z < SLOTS - 1)
            def _():
                copy_wait(lbuf.at[s, q, z], l_recv.at[s, q, z])
                prod[s, q, core, z] += lbuf[s, q, z]

            out_ref[s, :, cols] = prod[s, q, core, z].astype(BF16)

    def finish(s, q):
        for b in range(SLOTS):

            @pl.when(z < b)
            def _():
                line_copy(s, q, b, 2).wait_send()

            @pl.when(z > b)
            def _():
                line_copy(s, q, b, -2).wait_send()

    each(finish)


def per_device(queries, keys, values, token_gate, head_rate, init_state, norm_gain, out_proj, plan):
    seqs, rows, width = queries.shape
    heads = init_state.shape[0]
    pairs = seqs * heads
    model = out_proj.shape[1]
    vmem = pl.BlockSpec(memory_space=pltpu.VMEM)
    token_spec = pl.BlockSpec((1, rows, width), lambda s: (s, 0, 0))

    def pair_spec(a, b):
        return pl.BlockSpec((heads, a, b), lambda s: (s, 0, 0))

    fd, qh, ql, z0 = pl.pallas_call(
        local_kernel,
        grid=(seqs,),
        in_specs=[
            token_spec,
            token_spec,
            token_spec,
            pl.BlockSpec((1, heads, rows), lambda s: (s, 0, 0)),
            pl.BlockSpec(memory_space=pltpu.SMEM),
        ],
        out_specs=[pair_spec(HS, 2 * HS), pair_spec(rows, HS), pair_spec(rows, HS), pair_spec(rows, HS)],
        out_shape=[
            jax.ShapeDtypeStruct((pairs, HS, 2 * HS), F32),
            jax.ShapeDtypeStruct((pairs, rows, HS), BF16),
            jax.ShapeDtypeStruct((pairs, rows, HS), BF16),
            jax.ShapeDtypeStruct((pairs, rows, HS), F32),
        ],
        compiler_params=pltpu.CompilerParams(vmem_limit_bytes=40 * 2**20),
        name="slice_maps",
    )(queries, keys, values, token_gate, head_rate)

    dma = pltpu.SemaphoreType.DMA
    weights = pl.pallas_call(
        scan_kernel,
        out_shape=jax.ShapeDtypeStruct((pairs, HS, HS), F32),
        in_specs=[vmem] * 2,
        out_specs=vmem,
        scratch_shapes=[
            pltpu.VMEM((PLANE, HS, 2 * HS), F32),
            pltpu.VMEM((PLANE, HS, 2 * HS), F32),
            pltpu.VMEM((PLANE, HS, HS), F32),
            pltpu.VMEM((2, HS, HS), F32),
            pltpu.VMEM((pairs, HS, HS), F32),
            dma((pairs,)),
            dma((PLANE,)),
            dma((PLANE,)),
            dma((pairs,)),
            dma,
            dma,
        ],
        compiler_params=pltpu.CompilerParams(
            collective_id=0, has_side_effects=True, vmem_limit_bytes=24 * 2**20
        ),
        name="state_scan",
    )(fd, init_state)

    parts = 4
    cols = model // parts
    share = rows // (2 * SLOTS)
    line = pltpu.VMEM((seqs, parts, SLOTS, share, cols), F32)
    summed = pl.pallas_call(
        out_kernel,
        out_shape=jax.ShapeDtypeStruct((seqs, share, model), BF16),
        in_specs=[vmem] * 6,
        out_specs=vmem,
        scratch_shapes=[
            pltpu.VMEM((seqs, rows, width), BF16),
            pltpu.VMEM((seqs, parts, 2, SLOTS, share, cols), F32),
            line,
            line,
            line,
            dma((seqs, parts)),
            dma((seqs, parts)),
            dma((seqs, parts, SLOTS)),
            dma((seqs, parts, SLOTS)),
            dma((seqs, parts, SLOTS)),
            dma((seqs, parts, SLOTS)),
        ],
        compiler_params=pltpu.CompilerParams(
            collective_id=1, has_side_effects=True, vmem_limit_bytes=48 * 2**20
        ),
        name="project_sum",
    )(qh, ql, z0, weights, norm_gain.reshape(1, width), out_proj)
    straight = plan[0] == 0
    return jnp.stack(
        [jnp.where(straight, summed[0], summed[1]), jnp.where(straight, summed[1], summed[0])], axis=1
    )


def solution(mesh):
    return jax.shard_map(
        per_device,
        mesh=mesh,
        in_specs=(
            P(None, "ctx", "head"),
            P(None, "ctx", "head"),
            P(None, "ctx", "head"),
            P(None, "head", "ctx"),
            P("head"),
            P("head", None, None),
            P("head"),
            P("head", None),
            P(),
        ),
        out_specs=P(("ctx", "head"), None, None),
        check_vma=False,
    )
```

time: 1120 us -> 143 us (0.13)
  the two profiles are of different devices: /device:TPU:166 before, /device:TPU:158 now
where the time goes in v1:
time: 143 us
  Pallas kernels  135 us (94%)
  local copies, waits for them, and re-layouts  7.44 us (5%)
    pallas_call x1, Pallas kernels, per_device(): pl.pallas_call(out_kernel, out_shape=jax.ShapeDtypeStruct((seqs, share, m...  86.5 us
    pallas_call x1, Pallas kernels, per_device(): pl.pallas_call(scan_kernel, out_shape=jax.ShapeDtypeStruct((pairs, HS, HS...  41.9 us
    pallas_call x1, Pallas kernels, per_device(): pl.pallas_call(local_kernel, grid=(seqs,), in_specs=[token_spec, token_sp...  6.62 us
    unnamed x16, local copies, waits for them, and re-layouts  6.1 us

profile of v1, /device:TPU:158, one launch (start us, length us, event | category | flops | bytes accessed | tf_op | source)
XLA Modules:
  0.0 142.6 jit_solution(7497466681217478521)
XLA Ops:
  0.0 0.0 copy-start
  0.0 1.0 copy-done
  1.0 0.0 copy-start.1
  1.0 1.0 copy-done.1
  2.1 0.0 copy-start.2
  2.1 1.0 copy-done.2
  3.1 0.0 copy-start.4
  3.1 0.7 copy-done.4
  3.8 0.0 copy-start.6
  3.8 0.7 copy-done.6
  4.5 6.6 %slice_maps.1 = (f32[8,128,256]{2,1,0:T(8,128)S(1)}, bf16[8,256,128]{2,1,0:T(8,128)(2,1)S(1)}, bf16[8,256,128]{2,1,0:T(8,128)(2,1)S(1)}, f32[8,256,128]{2,1,0:T(8,128)S(1)}) custom-call(bf16[2,256,512]{2,1,0:T(8,128)(2,1)S(1)} %copy-done, bf16[2,256,512]{2,1,0:T(8,128)(2,1)S(1)} %copy-done.1, bf16[2,256,512]{2,1,0:T(8,128)(2,1)S(1)} %copy-done.2, ...), custom_call_target="tpu_custom_call" | custom-call | tf_op jit(solution)/shard_map/slice_maps/pallas_call | solution.py:381
  11.1 0.0 copy-start.3
  11.1 0.9 copy-done.3
  12.1 0.0 copy-start.7
  12.1 41.9 %state_scan.1.w_ref = f32[8,128,128]{2,1,0:T(8,128)S(1)} custom-call(f32[8,128,256]{2,1,0:T(8,128)S(1)} %get-tuple-element.12.fd_ref, f32[4,128,128]{2,1,0:T(8,128)S(1)} %copy-done.3), custom_call_target="tpu_custom_call" | custom-call | tf_op jit(solution)/shard_map/state_scan/pallas_call | solution.py:403
  53.9 0.0 copy-start.5
  53.9 0.7 copy-done.5
  54.6 86.5 %project_sum.1 = bf16[2,32,4096]{2,1,0:T(8,128)(2,1)S(1)} custom-call(bf16[8,256,128]{2,1,0:T(8,128)(2,1)S(1)} %get-tuple-element.9.qh_ref, bf16[8,256,128]{2,1,0:T(8,128)(2,1)S(1)} %get-tuple-element.10.ql_ref, f32[8,256,128]{2,1,0:T(8,128)S(1)} %get-tuple-element.11.z0_ref, f32[8,128,128]{2,1,0:T(8,128)S(1)} %state_scan.1.w_ref, f32[1,512]{1,0:T(1,128)S(1)} %bitcast.7, ...), custom_call_target="tpu_custom_call" | custom-call | tf_op jit(solution)/shard_map/project_sum/pallas_call | solution.py:431
  141.1 0.0 copy-done.7
  141.2 0.1 pad_maximum_fusion
  141.3 1.3 copy.10
  (1 shorter events, 0.0 us)
Async XLA Ops:
  0.0 1.0 copy-start
  1.0 1.0 copy-start.1
  2.1 1.0 copy-start.2
  3.1 0.7 copy-start.4
  3.8 0.7 copy-start.6
  11.1 1.0 copy-start.3
  12.1 129.1 %copy-start.7 = (s32[2]{0:T(128)S(1)}, s32[2]{0:T(128)}, u32[]{:S(2)}) copy-start(s32[2]{0:T(128)} %param.17) | copy-start | bytes 28
  53.9 0.7 copy-start.5

commit v2 on v0

v2 whole, which is shorter than its diff:
```python
import jax
import jax.numpy as jnp
from jax import lax
from jax.experimental import pallas as pl
from jax.experimental.pallas import tpu as pltpu
from jax.sharding import PartitionSpec as P

HS = 128
MB = 64
EPS = 1e-06
MESH = pl.DeviceIdType.MESH
F32 = jnp.float32
BF16 = jnp.bfloat16
PLANE = 16
SLOTS = 4


def halves(a):
    hi = a.astype(BF16)
    return hi, (a - hi.astype(F32)).astype(BF16)


def mm(a, b):
    return jnp.dot(a, b, preferred_element_type=F32)


def mm3(a, b):
    return mm(a[0], b[0]) + (mm(a[0], b[1]) + mm(a[1], b[0]))


def nt(a, b):
    return lax.dot_general(a, b, (((1,), (1,)), ((), ())), preferred_element_type=F32)


def tn(a, b):
    return lax.dot_general(a, b, (((0,), (0,)), ((), ())), preferred_element_type=F32)


def spread(k, v, ecol):
    rows = k.shape[0]
    gram = nt(k, k)
    kv = jnp.concatenate([k, v], axis=1).astype(F32)
    first = halves(kv[:MB] * ecol[:MB])
    his, los = [first[0]], [first[1]]
    for start in range(MB, rows, MB):
        left = halves(gram[start : start + MB, :start])
        hi, lo = jnp.concatenate(his, axis=0), jnp.concatenate(los, axis=0)
        part = kv[start : start + MB] - mm3(left, (hi, lo))
        nxt = halves(part * ecol[start : start + MB])
        his.append(nxt[0])
        los.append(nxt[1])
    return jnp.concatenate(his, axis=0), jnp.concatenate(los, axis=0)


def slice_map(k, hi, lo):
    moved = tn(k, hi) + tn(k, lo)
    r = lax.broadcasted_iota(jnp.int32, (HS, HS), 0)
    c = lax.broadcasted_iota(jnp.int32, (HS, HS), 1)
    eye = jnp.where(r == c, 1.0, 0.0).astype(F32)
    return jnp.concatenate([eye - moved[:, :HS], moved[:, HS:]], axis=1)


def readout(q, k, hi, lo):
    rows = q.shape[0]
    scores = nt(q, k)
    r = lax.broadcasted_iota(jnp.int32, (rows, rows), 0)
    c = lax.broadcasted_iota(jnp.int32, (rows, rows), 1)
    scores = halves(jnp.where(c <= r, scores, 0.0))
    read = mm3(scores, (hi, lo))
    return q.astype(F32) - read[:, :HS], read[:, HS:]


def after(earlier, later):
    moved = mm3(halves(later[:, :HS]), halves(earlier))
    return moved + jnp.concatenate([jnp.zeros((HS, HS), F32), later[:, HS:]], axis=1)


def applied(change, state):
    return mm3(halves(change[:, :HS]), halves(state)) + change[:, HS:]


def copy_wait(ref, sem):
    pltpu.make_async_copy(ref, ref, sem).wait()


def layer_kernel(
    q_hbm, k_hbm, v_hbm, gate_hbm, rate_hbm, init_hbm, gain_hbm, proj_hbm, out_ref,
    q_ref, k_ref, v_ref, gate_ref, rate_ref, init_ref, gain_ref, proj_ref,
    ehi, elo, fd_ref, qh_ref, ql_ref, z0_ref,
    recv, total, enter, wout, xw, wbuf, normed, prod, sib, rbuf, lbuf,
    in_sem, fd_send, fd_recv, w_send, w_recv, x_send, x_recv,
    sib_send, sib_recv, r_send, r_recv, l_send, l_recv,
):
    me_c, me_h = lax.axis_index("ctx"), lax.axis_index("head")
    zhi, p = me_c // PLANE, lax.rem(me_c, PLANE)
    x, y = p // 4, lax.rem(p, 4)
    z, core = me_h // 2, lax.rem(me_h, 2)
    twin = z * 2 + (1 - core)
    seqs, rows = q_ref.shape[0], q_ref.shape[1]
    heads = init_ref.shape[0]
    pairs = seqs * heads
    parts, width = prod.shape[1], prod.shape[-1]

    loads = []
    order = [(k_hbm.at[0], k_ref.at[0]), (v_hbm.at[0], v_ref.at[0]), (gate_hbm, gate_ref), (rate_hbm, rate_ref)]
    order += [(k_hbm.at[1], k_ref.at[1]), (v_hbm.at[1], v_ref.at[1]), (q_hbm, q_ref), (init_hbm, init_ref)]
    order += [(gain_hbm, gain_ref), (proj_hbm, proj_ref)]
    for i, (src, dst) in enumerate(order):
        loads.append(pltpu.make_async_copy(src, dst, in_sem.at[i]))
        loads[-1].start()

    barrier = pltpu.get_barrier_semaphore()
    for step in range(1, PLANE):
        other = zhi * PLANE + lax.rem(p + step, PLANE)
        pl.semaphore_signal(barrier, inc=1, device_id=(other, me_h), device_id_type=MESH)
    partner = (1 - zhi) * PLANE + p
    pl.semaphore_signal(barrier, inc=1, device_id=(partner, me_h), device_id_type=MESH)
    pl.semaphore_signal(barrier, inc=1, device_id=(me_c, twin), device_id_type=MESH)

    @pl.when(z > 0)
    def _():
        pl.semaphore_signal(barrier, inc=1, device_id=(me_c, me_h - 2), device_id_type=MESH)

    @pl.when(z < SLOTS - 1)
    def _():
        pl.semaphore_signal(barrier, inc=1, device_id=(me_c, me_h + 2), device_id_type=MESH)

    for i in range(4):
        loads[i].wait()
    etas = []
    for s in range(seqs):
        eta = [gate_ref[s, h : h + 1] * rate_ref[0:1, h : h + 1] for h in range(heads)]
        etas.append(jnp.concatenate(eta + [jnp.zeros((8 - heads, rows), F32)], axis=0).T)

    def home(s, h):
        return 4 * h + 2 * core + lax.rem(h + s, 2)

    def fd_copy(s, h):
        return pltpu.make_async_remote_copy(
            src_ref=fd_ref.at[s * heads + h],
            dst_ref=recv.at[p],
            send_sem=fd_send.at[s * heads + h],
            recv_sem=fd_recv.at[p],
            device_id=(zhi * PLANE + home(s, h), me_h),
            device_id_type=MESH,
        )

    for s in range(seqs):
        if s == 1:
            loads[4].wait()
            loads[5].wait()
        for h in range(heads):
            cols = slice(h * HS, (h + 1) * HS)
            k = k_ref[s, :, cols]
            hi, lo = spread(k, v_ref[s, :, cols], etas[s][:, h : h + 1])
            ehi[s * heads + h] = hi
            elo[s * heads + h] = lo
            fd_ref[s * heads + h] = slice_map(k, hi, lo)
        if s == 0:
            count = 2 + PLANE - 1 + jnp.where(z > 0, 1, 0) + jnp.where(z < SLOTS - 1, 1, 0)
            pl.semaphore_wait(barrier, count)
        for i in range(heads):
            h = lax.rem(x + i, heads)
            to = home(s, h)

            @pl.when(to != p)
            def _():
                fd_copy(s, h).start()

            @pl.when(to == p)
            def _():
                pltpu.make_async_copy(fd_ref.at[s * heads + h], recv.at[p], fd_recv.at[p]).start()

    loads[6].wait()
    for j in range(pairs):
        s, h = j // heads, j % heads
        cols = slice(h * HS, (h + 1) * HS)
        qt, z0 = readout(q_ref[s, :, cols], k_ref[s, :, cols], ehi[j], elo[j])
        hi, lo = halves(qt)
        qh_ref[j] = hi
        ql_ref[j] = lo
        z0_ref[j] = z0
    for load in loads[7:]:
        load.wait()

    handler = y // 2 == core
    mine = lax.rem(x + y, 2) * heads + x

    def w_copy(c):
        return pltpu.make_async_remote_copy(
            src_ref=wout.at[c],
            dst_ref=wbuf.at[mine],
            send_sem=w_send.at[c],
            recv_sem=w_recv.at[mine],
            device_id=(zhi * PLANE + c, me_h),
            device_id_type=MESH,
        )

    x_copy = pltpu.make_async_remote_copy(
        src_ref=xw.at[0],
        dst_ref=xw.at[1],
        send_sem=x_send,
        recv_sem=x_recv,
        device_id=(PLANE + p, me_h),
        device_id_type=MESH,
    )

    @pl.when(handler)
    def _():
        for i in range(4):
            for g in range(4):
                c = 4 * g + i
                copy_wait(recv.at[c], fd_recv.at[c])
                if i > 0:
                    recv[c] = after(recv[c - 1], recv[c])
        total[0] = recv[3]
        for g in range(1, 4):
            total[g] = after(total[g - 1], recv[4 * g + 3])

        @pl.when(zhi == 0)
        def _():
            enter[0] = init_ref[x]
            xw[0] = applied(total[3], init_ref[x])
            x_copy.start()

        @pl.when(zhi == 1)
        def _():
            x_copy.wait_recv()
            enter[0] = xw[1]

        for g in range(1, 4):
            enter[g] = applied(total[g - 1], enter[0])
        for i in range(4):
            g = lax.rem(x + i, 4)
            wout[4 * g] = enter[g]
            for k in range(1, 4):
                wout[4 * g + k] = applied(recv[4 * g + k - 1], enter[g])
            for k in range(4):
                c = 4 * g + k

                @pl.when(c != p)
                def _():
                    w_copy(c).start()

                @pl.when(c == p)
                def _():
                    pltpu.make_async_copy(wout.at[c], wbuf.at[mine], w_recv.at[mine]).start()

    def sib_copy(s, q):
        return pltpu.make_async_remote_copy(
            src_ref=prod.at[s, q, 1 - core],
            dst_ref=sib.at[s, q],
            send_sem=sib_send.at[s, q],
            recv_sem=sib_recv.at[s, q],
            device_id=(me_c, twin),
            device_id_type=MESH,
        )

    def line_copy(s, q, b, step):
        buf, send, got = (rbuf, r_send, r_recv) if step > 0 else (lbuf, l_send, l_recv)
        return pltpu.make_async_remote_copy(
            src_ref=prod.at[s, q, core, b],
            dst_ref=buf.at[s, q, b],
            send_sem=send.at[s, q, b],
            recv_sem=got.at[s, q, b],
            device_id=(me_c, me_h + step),
            device_id_type=MESH,
        )

    def each(body):
        lax.fori_loop(0, parts, lambda q, carry: (body(q), carry)[1], 0)

    def outputs(s):
        for h in range(heads):
            j = s * heads + h
            cols = slice(h * HS, (h + 1) * HS)
            copy_wait(wbuf.at[j], w_recv.at[j])
            zval = mm3((qh_ref[j], ql_ref[j]), halves(wbuf[j])) + z0_ref[j]
            scale = lax.rsqrt(jnp.mean(zval * zval, axis=-1, keepdims=True) + EPS)
            normed[s, :, cols] = (zval * scale * gain_ref[:, cols]).astype(BF16)

        def project(q):
            start = pl.multiple_of(q * width, width)
            part = mm(normed[s], proj_ref[:, pl.ds(start, width)])
            part = part.reshape(SLOTS, 2, rows // (2 * SLOTS), width)
            prod[s, q, 0] = part[:, 0]
            prod[s, q, 1] = part[:, 1]
            sib_copy(s, q).start()

        each(project)

    def pair_sums(s):
        def pair_sum(q):
            sib_copy(s, q).wait_recv()
            sib_copy(s, q).wait_send()
            for b in range(SLOTS):
                prod[s, q, core, b] += sib[s, q, b]

            @pl.when(z == 0)
            def _():
                for b in range(SLOTS - 1, 0, -1):
                    line_copy(s, q, b, 2).start()

            @pl.when(z == SLOTS - 1)
            def _():
                for b in range(SLOTS - 1):
                    line_copy(s, q, b, -2).start()

        each(pair_sum)

    def forwards(s):
        def forward(q):
            for b in range(SLOTS - 1, 0, -1):

                @pl.when(jnp.logical_and(z > 0, z < b))
                def _():
                    copy_wait(rbuf.at[s, q, b], r_recv.at[s, q, b])
                    prod[s, q, core, b] += rbuf[s, q, b]
                    line_copy(s, q, b, 2).start()

            for b in range(SLOTS - 1):

                @pl.when(jnp.logical_and(z < SLOTS - 1, z > b))
                def _():
                    copy_wait(lbuf.at[s, q, b], l_recv.at[s, q, b])
                    prod[s, q, core, b] += lbuf[s, q, b]
                    line_copy(s, q, b, -2).start()

        @pl.when(jnp.logical_and(z > 0, z < SLOTS - 1))
        def _():
            each(forward)

    outputs(0)
    pair_sums(0)
    outputs(1)
    forwards(0)
    pair_sums(1)
    forwards(1)

    for s in range(seqs):
        for q in range(parts):
            cols = slice(q * width, (q + 1) * width)

            @pl.when(z > 0)
            def _():
                copy_wait(rbuf.at[s, q, z], r_recv.at[s, q, z])
                prod[s, q, core, z] += rbuf[s, q, z]

            @pl.when(z < SLOTS - 1)
            def _():
                copy_wait(lbuf.at[s, q, z], l_recv.at[s, q, z])
                prod[s, q, core, z] += lbuf[s, q, z]

            out_ref[s, :, cols] = prod[s, q, core, z].astype(BF16)

    def finish(i, carry):
        s, q = i // parts, lax.rem(i, parts)
        for b in range(SLOTS):

            @pl.when(z < b)
            def _():
                line_copy(s, q, b, 2).wait_send()

            @pl.when(z > b)
            def _():
                line_copy(s, q, b, -2).wait_send()

        return carry

    lax.fori_loop(0, seqs * parts, finish, 0)
    for j in range(pairs):

        @pl.when(home(j // heads, j % heads) != p)
        def _():
            fd_copy(j // heads, j % heads).wait_send()

    @pl.when(handler)
    def _():
        def done(c, carry):
            @pl.when(c != p)
            def _():
                w_copy(c).wait_send()

            return carry

        lax.fori_loop(0, PLANE, done, 0)

        @pl.when(zhi == 0)
        def _():
            x_copy.wait_send()


def per_device(queries, keys, values, token_gate, head_rate, init_state, norm_gain, out_proj, plan):
    seqs, rows, width = queries.shape
    heads = init_state.shape[0]
    pairs = seqs * heads
    model = out_proj.shape[1]
    parts = 4
    cols = model // parts
    share = rows // (2 * SLOTS)
    dma = pltpu.SemaphoreType.DMA
    tokens = pltpu.VMEM((seqs, rows, width), BF16)
    line = pltpu.VMEM((seqs, parts, SLOTS, share, cols), F32)
    square = (HS, HS)
    summed = pl.pallas_call(
        layer_kernel,
        out_shape=jax.ShapeDtypeStruct((seqs, share, model), BF16),
        in_specs=[pl.BlockSpec(memory_space=pltpu.HBM)] * 8,
        out_specs=pl.BlockSpec(memory_space=pltpu.VMEM),
        scratch_shapes=[
            tokens,
            tokens,
            tokens,
            pltpu.VMEM((seqs, heads, rows), F32),
            pltpu.VMEM((1, heads), F32),
            pltpu.VMEM((heads,) + square, F32),
            pltpu.VMEM((1, width), F32),
            pltpu.VMEM((width, model), BF16),
            pltpu.VMEM((pairs, rows, 2 * HS), BF16),
            pltpu.VMEM((pairs, rows, 2 * HS), BF16),
            pltpu.VMEM((pairs, HS, 2 * HS), F32),
            pltpu.VMEM((pairs, rows, HS), BF16),
            pltpu.VMEM((pairs, rows, HS), BF16),
            pltpu.VMEM((pairs, rows, HS), F32),
            pltpu.VMEM((PLANE, HS, 2 * HS), F32),
            pltpu.VMEM((4, HS, 2 * HS), F32),
            pltpu.VMEM((4,) + square, F32),
            pltpu.VMEM((PLANE,) + square, F32),
            pltpu.VMEM((2,) + square, F32),
            pltpu.VMEM((pairs,) + square, F32),
            tokens,
            pltpu.VMEM((seqs, parts, 2, SLOTS, share, cols), F32),
            line,
            line,
            line,
            dma((10,)),
            dma((pairs,)),
            dma((PLANE,)),
            dma((PLANE,)),
            dma((pairs,)),
            dma,
            dma,
            dma((seqs, parts)),
            dma((seqs, parts)),
            dma((seqs, parts, SLOTS)),
            dma((seqs, parts, SLOTS)),
            dma((seqs, parts, SLOTS)),
            dma((seqs, parts, SLOTS)),
        ],
        compiler_params=pltpu.CompilerParams(
            collective_id=0, has_side_effects=True, vmem_limit_bytes=56 * 2**20
        ),
        name="layer",
    )(
        queries,
        keys,
        values,
        token_gate,
        head_rate.reshape(1, heads),
        init_state,
        norm_gain.reshape(1, width),
        out_proj,
    )
    straight = plan[0] == 0
    return jnp.stack(
        [jnp.where(straight, summed[0], summed[1]), jnp.where(straight, summed[1], summed[0])], axis=1
    )


def solution(mesh):
    return jax.shard_map(
        per_device,
        mesh=mesh,
        in_specs=(
            P(None, "ctx", "head"),
            P(None, "ctx", "head"),
            P(None, "ctx", "head"),
            P(None, "head", "ctx"),
            P("head"),
            P("head", None, None),
            P("head"),
            P("head", None),
            P(),
        ),
        out_specs=P(("ctx", "head"), None, None),
        check_vma=False,
    )
```

time: 1120 us -> 128 us (0.11)
  the two profiles are of different devices: /device:TPU:166 before, /device:TPU:144 now
where the time goes in v2:
time: 128 us
  Pallas kernels  124 us (97%)
  local copies, waits for them, and re-layouts  1.34 us (1%)
    pallas_call x1, Pallas kernels, per_device(): pl.pallas_call(layer_kernel, out_shape=jax.ShapeDtypeStruct((seqs, share,...  124 us

profile of v2, /device:TPU:144, one launch (start us, length us, event | category | flops | bytes accessed | tf_op | source)
XLA Modules:
  0.0 127.6 jit_solution(2971737118578116398)
XLA Ops:
  0.7 124.5 %layer.1 = bf16[2,32,4096]{2,1,0:T(8,128)(2,1)} custom-call(bf16[2,256,512]{2,1,0:T(8,128)(2,1)} %q_hbm.1, bf16[2,256,512]{2,1,0:T(8,128)(2,1)} %k_hbm.1, bf16[2,256,512]{2,1,0:T(8,128)(2,1)} %v_hbm.1, f32[2,4,256]{2,1,0:T(4,128)} %gate_hbm.1, f32[1,4]{1,0:T(1,128)} %bitcast.9, f32[4,128,128]{2,1,0:T(8,128)} %init_hbm.1, f32[1,512]{1,0:T(1,128)} %bitcast.8, ...), custom_call_target="tpu_custom_call" | custom-call | tf_op jit(solution)/shard_map/layer/pallas_call | solution.py:405
  125.1 1.1 select_bitcast_fusion.1
  126.2 0.1 pad_maximum_fusion
  126.3 1.3 %copy.10 = bf16[32,2,4096]{2,1,0:T(2,128)(2,1)} copy(bf16[32,2,4096]{2,0,1:T(8,128)(2,1)S(1)} %pad_maximum_fusion) | data formatting | bytes 1048576 | tf_op jit(solution)/shard_map/stack | solution.py:465

commit v3 on v2

--- a/solution.py
+++ b/solution.py
@@ -87,15 +87,21 @@
     q_hbm, k_hbm, v_hbm, gate_hbm, rate_hbm, init_hbm, gain_hbm, proj_hbm, out_ref,
     q_ref, k_ref, v_ref, gate_ref, rate_ref, init_ref, gain_ref, proj_ref,
     ehi, elo, fd_ref, qh_ref, ql_ref, z0_ref,
-    recv, total, enter, wout, xw, wbuf, normed, prod, sib, rbuf, lbuf,
+    recv, total, enter, wout, xw, wbuf, normed, prod, sib, rbuf, lbuf, nout, nin, eprod, esib,
     in_sem, fd_send, fd_recv, w_send, w_recv, x_send, x_recv,
-    sib_send, sib_recv, r_send, r_recv, l_send, l_recv,
+    sib_send, sib_recv, r_send, r_recv, l_send, l_recv, n_send, n_recv, e_send, e_recv,
 ):
     me_c, me_h = lax.axis_index("ctx"), lax.axis_index("head")
     zhi, p = me_c // PLANE, lax.rem(me_c, PLANE)
     x, y = p // 4, lax.rem(p, 4)
     z, core = me_h // 2, lax.rem(me_h, 2)
     twin = z * 2 + (1 - core)
+    partner = (1 - zhi) * PLANE + p
+    low, high = z == 0, z == SLOTS - 1
+    end = jnp.logical_or(low, high)
+    far = SLOTS - 1 - z
+    left = (jnp.where(low, partner, me_c), jnp.where(low, 2 * (SLOTS - 1) + core, me_h - 2))
+    right = (jnp.where(high, partner, me_c), jnp.where(high, core, me_h + 2))
     seqs, rows = q_ref.shape[0], q_ref.shape[1]
     heads = init_ref.shape[0]
     pairs = seqs * heads
@@ -113,17 +119,8 @@
     for step in range(1, PLANE):
         other = zhi * PLANE + lax.rem(p + step, PLANE)
         pl.semaphore_signal(barrier, inc=1, device_id=(other, me_h), device_id_type=MESH)
-    partner = (1 - zhi) * PLANE + p
-    pl.semaphore_signal(barrier, inc=1, device_id=(partner, me_h), device_id_type=MESH)
-    pl.semaphore_signal(barrier, inc=1, device_id=(me_c, twin), device_id_type=MESH)
-
-    @pl.when(z > 0)
-    def _():
-        pl.semaphore_signal(barrier, inc=1, device_id=(me_c, me_h - 2), device_id_type=MESH)
-
-    @pl.when(z < SLOTS - 1)
-    def _():
-        pl.semaphore_signal(barrier, inc=1, device_id=(me_c, me_h + 2), device_id_type=MESH)
+    for other in ((partner, me_h), (me_c, twin), left, right):
+        pl.semaphore_signal(barrier, inc=1, device_id=other, device_id_type=MESH)
 
     for i in range(4):
         loads[i].wait()
@@ -145,10 +142,7 @@
             device_id_type=MESH,
         )
 
-    for s in range(seqs):
-        if s == 1:
-            loads[4].wait()
-            loads[5].wait()
+    def send_maps(s):
         for h in range(heads):
             cols = slice(h * HS, (h + 1) * HS)
             k = k_ref[s, :, cols]
@@ -157,8 +151,7 @@
             elo[s * heads + h] = lo
             fd_ref[s * heads + h] = slice_map(k, hi, lo)
         if s == 0:
-            count = 2 + PLANE - 1 + jnp.where(z > 0, 1, 0) + jnp.where(z < SLOTS - 1, 1, 0)
-            pl.semaphore_wait(barrier, count)
+            pl.semaphore_wait(barrier, PLANE - 1 + 4)
         for i in range(heads):
             h = lax.rem(x + i, heads)
             to = home(s, h)
@@ -171,15 +164,23 @@
             def _():
                 pltpu.make_async_copy(fd_ref.at[s * heads + h], recv.at[p], fd_recv.at[p]).start()
 
+    def readouts(s):
+        for h in range(heads):
+            j = s * heads + h
+            cols = slice(h * HS, (h + 1) * HS)
+            qt, z0 = readout(q_ref[s, :, cols], k_ref[s, :, cols], ehi[j], elo[j])
+            hi, lo = halves(qt)
+            qh_ref[j] = hi
+            ql_ref[j] = lo
+            z0_ref[j] = z0
+
+    send_maps(0)
     loads[6].wait()
-    for j in range(pairs):
-        s, h = j // heads, j % heads
-        cols = slice(h * HS, (h + 1) * HS)
-        qt, z0 = readout(q_ref[s, :, cols], k_ref[s, :, cols], ehi[j], elo[j])
-        hi, lo = halves(qt)
-        qh_ref[j] = hi
-        ql_ref[j] = lo
-        z0_ref[j] = z0
+    readouts(0)
+    loads[4].wait()
+    loads[5].wait()
+    send_maps(1)
+    readouts(1)
     for load in loads[7:]:
         load.wait()
 
@@ -256,19 +257,48 @@
             device_id_type=MESH,
         )
 
-    def line_copy(s, q, b, step):
-        buf, send, got = (rbuf, r_send, r_recv) if step > 0 else (lbuf, l_send, l_recv)
+    def line_copy(s, q, b, src, toward_right):
+        buf, send, got = (rbuf, r_send, r_recv) if toward_right else (lbuf, l_send, l_recv)
         return pltpu.make_async_remote_copy(
-            src_ref=prod.at[s, q, core, b],
+            src_ref=src,
             dst_ref=buf.at[s, q, b],
             send_sem=send.at[s, q, b],
             recv_sem=got.at[s, q, b],
-            device_id=(me_c, me_h + step),
+            device_id=right if toward_right else left,
             device_id_type=MESH,
         )
 
+    def own_copy(s, q, b, toward_right):
+        return line_copy(s, q, b, prod.at[s, q, core, b], toward_right)
+
+    def far_copy(s, q, toward_right):
+        return line_copy(s, q, far, eprod.at[s, q, core], toward_right)
+
+    def rows_copy(s):
+        return pltpu.make_async_remote_copy(
+            src_ref=nout.at[s],
+            dst_ref=nin.at[s],
+            send_sem=n_send.at[s],
+            recv_sem=n_recv.at[s],
+            device_id=(partner, me_h),
+            device_id_type=MESH,
+        )
+
+    def twin_copy(s, q):
+        return pltpu.make_async_remote_copy(
+            src_ref=eprod.at[s, q, 1 - core],
+            dst_ref=esib.at[s, q],
+            send_sem=e_send.at[s, q],
+            recv_sem=e_recv.at[s, q],
+            device_id=(me_c, twin),
+            device_id_type=MESH,
+        )
+
     def each(body):
         lax.fori_loop(0, parts, lambda q, carry: (body(q), carry)[1], 0)
+
+    block = rows // SLOTS
+    half = block // 2
 
     def outputs(s):
         for h in range(heads):
@@ -279,10 +309,16 @@
             scale = lax.rsqrt(jnp.mean(zval * zval, axis=-1, keepdims=True) + EPS)
             normed[s, :, cols] = (zval * scale * gain_ref[:, cols]).astype(BF16)
 
+        @pl.when(end)
+        def _():
+            start = pl.multiple_of(far * block, block)
+            nout[s] = normed[s, pl.ds(start, block), :].astype(F32)
+            rows_copy(s).start()
+
         def project(q):
             start = pl.multiple_of(q * width, width)
             part = mm(normed[s], proj_ref[:, pl.ds(start, width)])
-            part = part.reshape(SLOTS, 2, rows // (2 * SLOTS), width)
+            part = part.reshape(SLOTS, 2, half, width)
             prod[s, q, 0] = part[:, 0]
             prod[s, q, 1] = part[:, 1]
             sib_copy(s, q).start()
@@ -298,76 +334,132 @@
 
             @pl.when(z == 0)
             def _():
-                for b in range(SLOTS - 1, 0, -1):
-                    line_copy(s, q, b, 2).start()
-
-            @pl.when(z == SLOTS - 1)
-            def _():
-                for b in range(SLOTS - 1):
-                    line_copy(s, q, b, -2).start()
+                own_copy(s, q, 2, True).start()
+                own_copy(s, q, 1, True).start()
+
+            @pl.when(z == 1)
+            def _():
+                own_copy(s, q, 3, True).start()
+
+            @pl.when(z == 2)
+            def _():
+                own_copy(s, q, 0, False).start()
+
+            @pl.when(z == 3)
+            def _():
+                own_copy(s, q, 1, False).start()
+                own_copy(s, q, 2, False).start()
 
         each(pair_sum)
 
+    def far_rows(s):
+        @pl.when(end)
+        def _():
+            copy_wait(nin.at[s], n_recv.at[s])
+            there = nin[s].astype(BF16)
+
+            def project(q):
+                start = pl.multiple_of(q * width, width)
+                part = mm(there, proj_ref[:, pl.ds(start, width)])
+                eprod[s, q] = part.reshape(2, half, width)
+                twin_copy(s, q).start()
+
+            each(project)
+
+            def pair_sum(q):
+                twin_copy(s, q).wait_recv()
+                eprod[s, q, core] += esib[s, q]
+
+                @pl.when(low)
+                def _():
+                    far_copy(s, q, False).start()
+
+                @pl.when(high)
+                def _():
+                    far_copy(s, q, True).start()
+
+            each(pair_sum)
+
+    def take(s, q, b, buf, got):
+        copy_wait(buf.at[s, q, b], got.at[s, q, b])
+        prod[s, q, core, b] += buf[s, q, b]
+
     def forwards(s):
-        def forward(q):
-            for b in range(SLOTS - 1, 0, -1):
-
-                @pl.when(jnp.logical_and(z > 0, z < b))
-                def _():
-                    copy_wait(rbuf.at[s, q, b], r_recv.at[s, q, b])
-                    prod[s, q, core, b] += rbuf[s, q, b]
-                    line_copy(s, q, b, 2).start()
-
-            for b in range(SLOTS - 1):
-
-                @pl.when(jnp.logical_and(z < SLOTS - 1, z > b))
-                def _():
-                    copy_wait(lbuf.at[s, q, b], l_recv.at[s, q, b])
-                    prod[s, q, core, b] += lbuf[s, q, b]
-                    line_copy(s, q, b, -2).start()
-
-        @pl.when(jnp.logical_and(z > 0, z < SLOTS - 1))
-        def _():
-            each(forward)
+        def up(q):
+            take(s, q, 2, rbuf, r_recv)
+            own_copy(s, q, 2, True).start()
+            take(s, q, 0, lbuf, l_recv)
+            own_copy(s, q, 0, False).start()
+
+        def down(q):
+            take(s, q, 1, lbuf, l_recv)
+            own_copy(s, q, 1, False).start()
+            take(s, q, 3, rbuf, r_recv)
+            own_copy(s, q, 3, True).start()
+
+        @pl.when(z == 1)
+        def _():
+            each(up)
+
+        @pl.when(z == 2)
+        def _():
+            each(down)
 
     outputs(0)
     pair_sums(0)
+    far_rows(0)
     outputs(1)
     forwards(0)
     pair_sums(1)
+    far_rows(1)
     forwards(1)
 
     for s in range(seqs):
         for q in range(parts):
-            cols = slice(q * width, (q + 1) * width)
-
-            @pl.when(z > 0)
-            def _():
-                copy_wait(rbuf.at[s, q, z], r_recv.at[s, q, z])
-                prod[s, q, core, z] += rbuf[s, q, z]
-
-            @pl.when(z < SLOTS - 1)
-            def _():
-                copy_wait(lbuf.at[s, q, z], l_recv.at[s, q, z])
-                prod[s, q, core, z] += lbuf[s, q, z]
-
-            out_ref[s, :, cols] = prod[s, q, core, z].astype(BF16)
+            take(s, q, z, rbuf, r_recv)
+            take(s, q, z, lbuf, l_recv)
+            out_ref[s, :, q * width : (q + 1) * width] = prod[s, q, core, z].astype(BF16)
 
     def finish(i, carry):
         s, q = i // parts, lax.rem(i, parts)
-        for b in range(SLOTS):
-
-            @pl.when(z < b)
-            def _():
-                line_copy(s, q, b, 2).wait_send()
-
-            @pl.when(z > b)
-            def _():
-                line_copy(s, q, b, -2).wait_send()
+
+        @pl.when(z == 0)
+        def _():
+            own_copy(s, q, 2, True).wait_send()
+            own_copy(s, q, 1, True).wait_send()
+            far_copy(s, q, False).wait_send()
+
+        @pl.when(z == 1)
+        def _():
+            own_copy(s, q, 3, True).wait_send()
+            own_copy(s, q, 2, True).wait_send()
+            own_copy(s, q, 0, False).wait_send()
+
+        @pl.when(z == 2)
+        def _():
+            own_copy(s, q, 0, False).wait_send()
+            own_copy(s, q, 1, False).wait_send()
+            own_copy(s, q, 3, True).wait_send()
+
+        @pl.when(z == 3)
+        def _():
+            own_copy(s, q, 1, False).wait_send()
+            own_copy(s, q, 2, False).wait_send()
+            far_copy(s, q, True).wait_send()
+
+        @pl.when(end)
+        def _():
+            twin_copy(s, q).wait_send()
 
         return carry
 
     lax.fori_loop(0, seqs * parts, finish, 0)
+
+    @pl.when(end)
+    def _():
+        for s in range(seqs):
+            rows_copy(s).wait_send()
+
     for j in range(pairs):
 
         @pl.when(home(j // heads, j % heads) != p)
@@ -433,6 +525,10 @@
             line,
             line,
             line,
+            pltpu.VMEM((seqs, rows // SLOTS, width), F32),
+            pltpu.VMEM((seqs, rows // SLOTS, width), F32),
+            pltpu.VMEM((seqs, parts, 2, share, cols), F32),
+            pltpu.VMEM((seqs, parts, share, cols), F32),
             dma((10,)),
             dma((pairs,)),
             dma((PLANE,)),
@@ -446,6 +542,10 @@
             dma((seqs, parts, SLOTS)),
             dma((seqs, parts, SLOTS)),
             dma((seqs, parts, SLOTS)),
+            dma((seqs,)),
+            dma((seqs,)),
+            dma((seqs, parts)),
+            dma((seqs, parts)),
         ],
         compiler_params=pltpu.CompilerParams(
             collective_id=0, has_side_effects=True, vmem_limit_bytes=56 * 2**20

time: 128 us -> 100 us (0.78)
  the two profiles are of different devices: /device:TPU:144 before, /device:TPU:240 now
where the time goes in v3:
time: 100 us
  Pallas kernels  97.3 us (97%)
  local copies, waits for them, and re-layouts  1.34 us (1%)
  other arithmetic  1.12 us (1%)
    pallas_call x1, Pallas kernels, per_device(): pl.pallas_call(layer_kernel, out_shape=jax.ShapeDtypeStruct((seqs, share,...  97.3 us

profile of v3, /device:TPU:240, one launch (start us, length us, event | category | flops | bytes accessed | tf_op | source)
XLA Modules:
  0.0 100.4 jit_solution(17823318123819645496)
XLA Ops:
  0.7 97.3 %layer.1 = bf16[2,32,4096]{2,1,0:T(8,128)(2,1)} custom-call(bf16[2,256,512]{2,1,0:T(8,128)(2,1)} %q_hbm.1, bf16[2,256,512]{2,1,0:T(8,128)(2,1)} %k_hbm.1, bf16[2,256,512]{2,1,0:T(8,128)(2,1)} %v_hbm.1, f32[2,4,256]{2,1,0:T(4,128)} %gate_hbm.1, f32[1,4]{1,0:T(1,128)} %bitcast.9, f32[4,128,128]{2,1,0:T(8,128)} %init_hbm.1, f32[1,512]{1,0:T(1,128)} %bitcast.8, ...), custom_call_target="tpu_custom_call" | custom-call | tf_op jit(solution)/shard_map/layer/pallas_call | solution.py:497
  97.9 1.1 %select_bitcast_fusion.1 = (bf16[32,1,4096]{2,0,1:T(8,128)(2,1)S(1)}, bf16[32,1,4096]{2,0,1:T(8,128)(2,1)S(1)}) fusion(pred[]{:T(512)} %bitcast, bf16[2,32,4096]{2,1,0:T(8,128)(2,1)} %layer.1), kind=kLoop, calls=%fused_computation.2 | loop fusion | flops 262144 | bytes 1048577 | tf_op jit(solution)/shard_map/jit(_where)/select_n | solution.py:566
  99.0 0.1 pad_maximum_fusion
  99.1 1.3 %copy.10 = bf16[32,2,4096]{2,1,0:T(2,128)(2,1)} copy(bf16[32,2,4096]{2,0,1:T(8,128)(2,1)S(1)} %pad_maximum_fusion) | data formatting | bytes 1048576 | tf_op jit(solution)/shard_map/stack | solution.py:565

commit v4 on v3

--- a/solution.py
+++ b/solution.py
@@ -12,6 +12,8 @@
 F32 = jnp.float32
 BF16 = jnp.bfloat16
 PLANE = 16
+SIDE = 4
+HALF = 8
 SLOTS = 4
 
 
@@ -87,13 +89,18 @@
     q_hbm, k_hbm, v_hbm, gate_hbm, rate_hbm, init_hbm, gain_hbm, proj_hbm, out_ref,
     q_ref, k_ref, v_ref, gate_ref, rate_ref, init_ref, gain_ref, proj_ref,
     ehi, elo, fd_ref, qh_ref, ql_ref, z0_ref,
-    recv, total, enter, wout, xw, wbuf, normed, prod, sib, rbuf, lbuf, nout, nin, eprod, esib,
-    in_sem, fd_send, fd_recv, w_send, w_recv, x_send, x_recv,
+    recv, total, enter, wout, chain, wbuf, normed, prod, sib, rbuf, lbuf, nout, nin, eprod, esib,
+    in_sem, fd_send, fd_recv, w_send, w_recv, c_send, c_recv, t_send, t_recv,
     sib_send, sib_recv, r_send, r_recv, l_send, l_recv, n_send, n_recv, e_send, e_recv,
 ):
     me_c, me_h = lax.axis_index("ctx"), lax.axis_index("head")
     zhi, p = me_c // PLANE, lax.rem(me_c, PLANE)
-    x, y = p // 4, lax.rem(p, 4)
+    x, y = p // SIDE, lax.rem(p, SIDE)
+    near, spot = x // 2, lax.rem(p, HALF)
+    base = zhi * PLANE + near * HALF
+    stage = 2 * zhi + near
+    across = zhi * PLANE + lax.rem(p + HALF, PLANE)
+    far_across = (1 - zhi) * PLANE + lax.rem(p + HALF, PLANE)
     z, core = me_h // 2, lax.rem(me_h, 2)
     twin = z * 2 + (1 - core)
     partner = (1 - zhi) * PLANE + p
@@ -116,10 +123,10 @@
         loads[-1].start()
 
     barrier = pltpu.get_barrier_semaphore()
-    for step in range(1, PLANE):
-        other = zhi * PLANE + lax.rem(p + step, PLANE)
+    for step in range(1, HALF):
+        other = base + lax.rem(spot + step, HALF)
         pl.semaphore_signal(barrier, inc=1, device_id=(other, me_h), device_id_type=MESH)
-    for other in ((partner, me_h), (me_c, twin), left, right):
+    for other in ((partner, me_h), (across, me_h), (far_across, me_h), (me_c, twin), left, right):
         pl.semaphore_signal(barrier, inc=1, device_id=other, device_id_type=MESH)
 
     for i in range(4):
@@ -130,19 +137,19 @@
         etas.append(jnp.concatenate(eta + [jnp.zeros((8 - heads, rows), F32)], axis=0).T)
 
     def home(s, h):
-        return 4 * h + 2 * core + lax.rem(h + s, 2)
+        return (core if s == 0 else 1 - core) * SIDE + h
 
     def fd_copy(s, h):
         return pltpu.make_async_remote_copy(
             src_ref=fd_ref.at[s * heads + h],
-            dst_ref=recv.at[p],
+            dst_ref=recv.at[spot],
             send_sem=fd_send.at[s * heads + h],
-            recv_sem=fd_recv.at[p],
-            device_id=(zhi * PLANE + home(s, h), me_h),
+            recv_sem=fd_recv.at[spot],
+            device_id=(base + home(s, h), me_h),
             device_id_type=MESH,
         )
 
-    def send_maps(s):
+    def make_maps(s):
         for h in range(heads):
             cols = slice(h * HS, (h + 1) * HS)
             k = k_ref[s, :, cols]
@@ -150,19 +157,19 @@
             ehi[s * heads + h] = hi
             elo[s * heads + h] = lo
             fd_ref[s * heads + h] = slice_map(k, hi, lo)
-        if s == 0:
-            pl.semaphore_wait(barrier, PLANE - 1 + 4)
+
+    def send_maps(s):
         for i in range(heads):
-            h = lax.rem(x + i, heads)
+            h = lax.rem(y + i, heads)
             to = home(s, h)
 
-            @pl.when(to != p)
+            @pl.when(to != spot)
             def _():
                 fd_copy(s, h).start()
 
-            @pl.when(to == p)
-            def _():
-                pltpu.make_async_copy(fd_ref.at[s * heads + h], recv.at[p], fd_recv.at[p]).start()
+            @pl.when(to == spot)
+            def _():
+                pltpu.make_async_copy(fd_ref.at[s * heads + h], recv.at[spot], fd_recv.at[spot]).start()
 
     def readouts(s):
         for h in range(heads):
@@ -174,18 +181,20 @@
             ql_ref[j] = lo
             z0_ref[j] = z0
 
+    make_maps(0)
+    pl.semaphore_wait(barrier, HALF - 1 + 6)
     send_maps(0)
     loads[6].wait()
     readouts(0)
     loads[4].wait()
     loads[5].wait()
-    send_maps(1)
+    make_maps(1)
     readouts(1)
     for load in loads[7:]:
         load.wait()
 
-    handler = y // 2 == core
-    mine = lax.rem(x + y, 2) * heads + x
+    first = lax.rem(x, 2) == core
+    mine = jnp.where(first, 0, heads) + y
 
     def w_copy(c):
         return pltpu.make_async_remote_copy(
@@ -193,59 +202,82 @@
             dst_ref=wbuf.at[mine],
             send_sem=w_send.at[c],
             recv_sem=w_recv.at[mine],
-            device_id=(zhi * PLANE + c, me_h),
+            device_id=(base + c, me_h),
             device_id_type=MESH,
         )
 
-    x_copy = pltpu.make_async_remote_copy(
-        src_ref=xw.at[0],
-        dst_ref=xw.at[1],
-        send_sem=x_send,
-        recv_sem=x_recv,
-        device_id=(PLANE + p, me_h),
+    def chain_copy(i, to):
+        return pltpu.make_async_remote_copy(
+            src_ref=chain.at[0],
+            dst_ref=chain.at[1],
+            send_sem=c_send.at[i],
+            recv_sem=c_recv,
+            device_id=(to, me_h),
+            device_id_type=MESH,
+        )
+
+    t_copy = pltpu.make_async_remote_copy(
+        src_ref=total.at[0],
+        dst_ref=total.at[1],
+        send_sem=t_send,
+        recv_sem=t_recv,
+        device_id=(across, me_h),
         device_id_type=MESH,
     )
 
-    @pl.when(handler)
-    def _():
-        for i in range(4):
-            for g in range(4):
-                c = 4 * g + i
-                copy_wait(recv.at[c], fd_recv.at[c])
-                if i > 0:
-                    recv[c] = after(recv[c - 1], recv[c])
-        total[0] = recv[3]
-        for g in range(1, 4):
-            total[g] = after(total[g - 1], recv[4 * g + 3])
-
-        @pl.when(zhi == 0)
-        def _():
-            enter[0] = init_ref[x]
-            xw[0] = applied(total[3], init_ref[x])
-            x_copy.start()
-
-        @pl.when(zhi == 1)
-        def _():
-            x_copy.wait_recv()
-            enter[0] = xw[1]
-
-        for g in range(1, 4):
-            enter[g] = applied(total[g - 1], enter[0])
-        for i in range(4):
-            g = lax.rem(x + i, 4)
-            wout[4 * g] = enter[g]
-            for k in range(1, 4):
-                wout[4 * g + k] = applied(recv[4 * g + k - 1], enter[g])
-            for k in range(4):
-                c = 4 * g + k
-
-                @pl.when(c != p)
-                def _():
-                    w_copy(c).start()
-
-                @pl.when(c == p)
-                def _():
-                    pltpu.make_async_copy(wout.at[c], wbuf.at[mine], w_recv.at[mine]).start()
+    def scan(s):
+        @pl.when(first if s == 0 else jnp.logical_not(first))
+        def _():
+            for i in range(SIDE):
+                for g in range(2):
+                    c = SIDE * g + i
+                    copy_wait(recv.at[c], fd_recv.at[c])
+                    if i > 0:
+                        recv[c] = after(recv[c - 1], recv[c])
+            total[0] = after(recv[SIDE - 1], recv[HALF - 1])
+
+            @pl.when(stage == 2)
+            def _():
+                t_copy.start()
+
+            @pl.when(stage == 0)
+            def _():
+                enter[0] = init_ref[y]
+                chain[0] = applied(total[0], init_ref[y])
+                chain_copy(0, across).start()
+
+            @pl.when(stage > 0)
+            def _():
+                copy_wait(chain.at[1], c_recv)
+                enter[0] = chain[1]
+
+            @pl.when(stage == 1)
+            def _():
+                chain[0] = applied(total[0], enter[0])
+                chain_copy(0, far_across).start()
+                chain_copy(1, partner).start()
+
+            @pl.when(stage == 3)
+            def _():
+                t_copy.wait_recv()
+                enter[0] = applied(total[1], chain[1])
+
+            enter[1] = applied(recv[SIDE - 1], enter[0])
+            for i in range(2):
+                g = lax.rem(x + i, 2)
+                wout[SIDE * g] = enter[g]
+                for k in range(1, SIDE):
+                    wout[SIDE * g + k] = applied(recv[SIDE * g + k - 1], enter[g])
+                for i2 in range(SIDE):
+                    c = SIDE * g + lax.rem(y + i2, SIDE)
+
+                    @pl.when(c != spot)
+                    def _():
+                        w_copy(c).start()
+
+                    @pl.when(c == spot)
+                    def _():
+                        pltpu.make_async_copy(wout.at[c], wbuf.at[mine], w_recv.at[mine]).start()
 
     def sib_copy(s, q):
         return pltpu.make_async_remote_copy(
@@ -301,10 +333,13 @@
     half = block // 2
 
     def outputs(s):
+        for j in range(s * heads, (s + 1) * heads):
+            copy_wait(wbuf.at[j], w_recv.at[j])
+        if s == 0:
+            send_maps(1)
         for h in range(heads):
             j = s * heads + h
             cols = slice(h * HS, (h + 1) * HS)
-            copy_wait(wbuf.at[j], w_recv.at[j])
             zval = mm3((qh_ref[j], ql_ref[j]), halves(wbuf[j])) + z0_ref[j]
             scale = lax.rsqrt(jnp.mean(zval * zval, axis=-1, keepdims=True) + EPS)
             normed[s, :, cols] = (zval * scale * gain_ref[:, cols]).astype(BF16)
@@ -323,9 +358,6 @@
             prod[s, q, 1] = part[:, 1]
             sib_copy(s, q).start()
 
-        each(project)
-
-    def pair_sums(s):
         def pair_sum(q):
             sib_copy(s, q).wait_recv()
             sib_copy(s, q).wait_send()
@@ -335,7 +367,6 @@
             @pl.when(z == 0)
             def _():
                 own_copy(s, q, 2, True).start()
-                own_copy(s, q, 1, True).start()
 
             @pl.when(z == 1)
             def _():
@@ -348,9 +379,31 @@
             @pl.when(z == 3)
             def _():
                 own_copy(s, q, 1, False).start()
-                own_copy(s, q, 2, False).start()
-
-        each(pair_sum)
+
+        def both(q):
+            project(q)
+            pair_sum(q - 1)
+
+        project(0)
+        lax.fori_loop(1, parts, lambda q, carry: (both(q), carry)[1], 0)
+        pair_sum(parts - 1)
+
+    def nearest(s):
+        def rightward(q):
+            own_copy(s, q, 2, True).wait_send()
+            own_copy(s, q, 1, True).start()
+
+        def leftward(q):
+            own_copy(s, q, 1, False).wait_send()
+            own_copy(s, q, 2, False).start()
+
+        @pl.when(z == 0)
+        def _():
+            each(rightward)
+
+        @pl.when(z == 3)
+        def _():
+            each(leftward)
 
     def far_rows(s):
         @pl.when(end)
@@ -405,27 +458,30 @@
         def _():
             each(down)
 
-    outputs(0)
-    pair_sums(0)
-    far_rows(0)
-    outputs(1)
-    forwards(0)
-    pair_sums(1)
-    far_rows(1)
-    forwards(1)
-
-    for s in range(seqs):
+    def finals(s):
         for q in range(parts):
             take(s, q, z, rbuf, r_recv)
             take(s, q, z, lbuf, l_recv)
             out_ref[s, :, q * width : (q + 1) * width] = prod[s, q, core, z].astype(BF16)
 
+    scan(0)
+    outputs(0)
+    far_rows(0)
+    scan(1)
+    nearest(0)
+    forwards(0)
+    outputs(1)
+    far_rows(1)
+    nearest(1)
+    finals(0)
+    forwards(1)
+    finals(1)
+
     def finish(i, carry):
         s, q = i // parts, lax.rem(i, parts)
 
         @pl.when(z == 0)
         def _():
-            own_copy(s, q, 2, True).wait_send()
             own_copy(s, q, 1, True).wait_send()
             far_copy(s, q, False).wait_send()
 
@@ -443,7 +499,6 @@
 
         @pl.when(z == 3)
         def _():
-            own_copy(s, q, 1, False).wait_send()
             own_copy(s, q, 2, False).wait_send()
             far_copy(s, q, True).wait_send()
 
@@ -462,24 +517,31 @@
 
     for j in range(pairs):
 
-        @pl.when(home(j // heads, j % heads) != p)
+        @pl.when(home(j // heads, j % heads) != spot)
         def _():
             fd_copy(j // heads, j % heads).wait_send()
 
-    @pl.when(handler)
+    def done(c, carry):
+        @pl.when(c != spot)
+        def _():
+            w_copy(c).wait_send()
+
+        return carry
+
+    lax.fori_loop(0, HALF, done, 0)
+
+    @pl.when(stage == 0)
     def _():
-        def done(c, carry):
-            @pl.when(c != p)
-            def _():
-                w_copy(c).wait_send()
-
-            return carry
-
-        lax.fori_loop(0, PLANE, done, 0)
-
-        @pl.when(zhi == 0)
-        def _():
-            x_copy.wait_send()
+        chain_copy(0, across).wait_send()
+
+    @pl.when(stage == 1)
+    def _():
+        chain_copy(0, far_across).wait_send()
+        chain_copy(1, partner).wait_send()
+
+    @pl.when(stage == 2)
+    def _():
+        t_copy.wait_send()
 
 
 def per_device(queries, keys, values, token_gate, head_rate, init_state, norm_gain, out_proj, plan):
@@ -514,10 +576,10 @@
             pltpu.VMEM((pairs, rows, HS), BF16),
             pltpu.VMEM((pairs, rows, HS), BF16),
             pltpu.VMEM((pairs, rows, HS), F32),
-            pltpu.VMEM((PLANE, HS, 2 * HS), F32),
-            pltpu.VMEM((4, HS, 2 * HS), F32),
-            pltpu.VMEM((4,) + square, F32),
-            pltpu.VMEM((PLANE,) + square, F32),
+            pltpu.VMEM((HALF, HS, 2 * HS), F32),
+            pltpu.VMEM((2, HS, 2 * HS), F32),
+            pltpu.VMEM((2,) + square, F32),
+            pltpu.VMEM((HALF,) + square, F32),
             pltpu.VMEM((2,) + square, F32),
             pltpu.VMEM((pairs,) + square, F32),
             tokens,
@@ -531,9 +593,11 @@
             pltpu.VMEM((seqs, parts, share, cols), F32),
             dma((10,)),
             dma((pairs,)),
-            dma((PLANE,)),
-            dma((PLANE,)),
+            dma((HALF,)),
+            dma((HALF,)),
             dma((pairs,)),
+            dma((2,)),
+            dma,
             dma,
             dma,
             dma((seqs, parts)),

time: 100 us -> 95.9 us (0.959)
  the two profiles are of different devices: /device:TPU:240 before, /device:TPU:166 now
where the time goes in v4:
time: 95.9 us; the launch traced here: 94.5 us
  Pallas kernels  91.3 us (95%)
  local copies, waits for them, and re-layouts  1.34 us (1%)
  other arithmetic  1.12 us (1%)
    pallas_call x1, Pallas kernels, per_device(): pl.pallas_call(layer_kernel, out_shape=jax.ShapeDtypeStruct((seqs, share,...  91.3 us

profile of v4, /device:TPU:166, one launch (start us, length us, event | category | flops | bytes accessed | tf_op | source)
XLA Modules:
  0.0 94.5 jit_solution(14863784544654000481)
XLA Ops:
  0.7 91.3 %layer.1 = bf16[2,32,4096]{2,1,0:T(8,128)(2,1)} custom-call(bf16[2,256,512]{2,1,0:T(8,128)(2,1)} %q_hbm.1, bf16[2,256,512]{2,1,0:T(8,128)(2,1)} %k_hbm.1, bf16[2,256,512]{2,1,0:T(8,128)(2,1)} %v_hbm.1, f32[2,4,256]{2,1,0:T(4,128)} %gate_hbm.1, f32[1,4]{1,0:T(1,128)} %bitcast.9, f32[4,128,128]{2,1,0:T(8,128)} %init_hbm.1, f32[1,512]{1,0:T(1,128)} %bitcast.8, ...), custom_call_target="tpu_custom_call" | custom-call | tf_op jit(solution)/shard_map/layer/pallas_call | solution.py:559
  92.0 1.1 %select_bitcast_fusion.1 = (bf16[32,1,4096]{2,0,1:T(8,128)(2,1)S(1)}, bf16[32,1,4096]{2,0,1:T(8,128)(2,1)S(1)}) fusion(pred[]{:T(512)} %bitcast, bf16[2,32,4096]{2,1,0:T(8,128)(2,1)} %layer.1), kind=kLoop, calls=%fused_computation.2 | loop fusion | flops 262144 | bytes 1048577 | tf_op jit(solution)/shard_map/jit(_where)/select_n | solution.py:630
  93.1 0.1 pad_maximum_fusion
  93.1 1.3 %copy.10 = bf16[32,2,4096]{2,1,0:T(2,128)(2,1)} copy(bf16[32,2,4096]{2,0,1:T(8,128)(2,1)S(1)} %pad_maximum_fusion) | data formatting | bytes 1048576 | tf_op jit(solution)/shard_map/stack | solution.py:629

commit v5 on v4

--- a/solution.py
+++ b/solution.py
@@ -86,11 +86,11 @@
 
 
 def layer_kernel(
-    q_hbm, k_hbm, v_hbm, gate_hbm, rate_hbm, init_hbm, gain_hbm, proj_hbm, out_ref,
-    q_ref, k_ref, v_ref, gate_ref, rate_ref, init_ref, gain_ref, proj_ref,
+    q_hbm, k_hbm, v_hbm, gate_hbm, rate_hbm, init_hbm, gain_hbm, plan_hbm, proj_hbm, out_ref,
+    q_ref, k_ref, v_ref, gate_ref, rate_ref, init_ref, gain_ref, plan_ref, proj_ref,
     ehi, elo, fd_ref, qh_ref, ql_ref, z0_ref,
-    recv, total, enter, wout, chain, wbuf, normed, prod, sib, rbuf, lbuf, nout, nin, eprod, esib,
-    in_sem, fd_send, fd_recv, w_send, w_recv, c_send, c_recv, t_send, t_recv,
+    done_first, recv, total, enter, wout, chain, wbuf, normed, prod, sib, rbuf, lbuf, nout, nin, eprod, esib,
+    in_sem, fd_send, fd_recv, w_send, w_recv, c_send, c_recv, t_send, t_recv, m_send, m_recv,
     sib_send, sib_recv, r_send, r_recv, l_send, l_recv, n_send, n_recv, e_send, e_recv,
 ):
     me_c, me_h = lax.axis_index("ctx"), lax.axis_index("head")
@@ -117,7 +117,7 @@
     loads = []
     order = [(k_hbm.at[0], k_ref.at[0]), (v_hbm.at[0], v_ref.at[0]), (gate_hbm, gate_ref), (rate_hbm, rate_ref)]
     order += [(k_hbm.at[1], k_ref.at[1]), (v_hbm.at[1], v_ref.at[1]), (q_hbm, q_ref), (init_hbm, init_ref)]
-    order += [(gain_hbm, gain_ref), (proj_hbm, proj_ref)]
+    order += [(gain_hbm, gain_ref), (plan_hbm, plan_ref), (proj_hbm, proj_ref)]
     for i, (src, dst) in enumerate(order):
         loads.append(pltpu.make_async_copy(src, dst, in_sem.at[i]))
         loads[-1].start()
@@ -216,6 +216,16 @@
             device_id_type=MESH,
         )
 
+    def map_copy(i, to):
+        return pltpu.make_async_remote_copy(
+            src_ref=total.at[0],
+            dst_ref=total.at[2],
+            send_sem=m_send.at[i],
+            recv_sem=m_recv,
+            device_id=(to, me_h),
+            device_id_type=MESH,
+        )
+
     t_copy = pltpu.make_async_remote_copy(
         src_ref=total.at[0],
         dst_ref=total.at[1],
@@ -244,23 +254,42 @@
             def _():
                 enter[0] = init_ref[y]
                 chain[0] = applied(total[0], init_ref[y])
+                if s == 0:
+                    chain_copy(1, far_across).start()
+                    chain_copy(2, partner).start()
                 chain_copy(0, across).start()
+
+            if s == 0:
+
+                @pl.when(stage == 1)
+                def _():
+                    map_copy(0, far_across).start()
+                    map_copy(1, partner).start()
 
             @pl.when(stage > 0)
             def _():
                 copy_wait(chain.at[1], c_recv)
                 enter[0] = chain[1]
 
-            @pl.when(stage == 1)
-            def _():
-                chain[0] = applied(total[0], enter[0])
-                chain_copy(0, far_across).start()
-                chain_copy(1, partner).start()
+            if s == 0:
+
+                @pl.when(stage > 1)
+                def _():
+                    copy_wait(total.at[2], m_recv)
+                    enter[0] = applied(total[2], chain[1])
+
+            else:
+
+                @pl.when(stage == 1)
+                def _():
+                    chain[0] = applied(total[0], enter[0])
+                    chain_copy(0, far_across).start()
+                    chain_copy(1, partner).start()
 
             @pl.when(stage == 3)
             def _():
                 t_copy.wait_recv()
-                enter[0] = applied(total[1], chain[1])
+                enter[0] = applied(total[1], enter[0])
 
             enter[1] = applied(recv[SIDE - 1], enter[0])
             for i in range(2):
@@ -462,7 +491,15 @@
         for q in range(parts):
             take(s, q, z, rbuf, r_recv)
             take(s, q, z, lbuf, l_recv)
-            out_ref[s, :, q * width : (q + 1) * width] = prod[s, q, core, z].astype(BF16)
+            value = prod[s, q, core, z]
+            cols = slice(q * width, (q + 1) * width)
+            if s == 0:
+                done_first[:, cols] = value
+            else:
+                other = done_first[:, cols]
+                straight = plan_ref[0:1, 0:1] == 0
+                out_ref[:, 0, cols] = jnp.where(straight, other, value)
+                out_ref[:, 1, cols] = jnp.where(straight, value, other)
 
     scan(0)
     outputs(0)
@@ -534,7 +571,17 @@
     def _():
         chain_copy(0, across).wait_send()
 
-    @pl.when(stage == 1)
+        @pl.when(first)
+        def _():
+            chain_copy(1, far_across).wait_send()
+            chain_copy(2, partner).wait_send()
+
+    @pl.when(jnp.logical_and(stage == 1, first))
+    def _():
+        map_copy(0, far_across).wait_send()
+        map_copy(1, partner).wait_send()
+
+    @pl.when(jnp.logical_and(stage == 1, jnp.logical_not(first)))
     def _():
         chain_copy(0, far_across).wait_send()
         chain_copy(1, partner).wait_send()
@@ -558,8 +605,8 @@
     square = (HS, HS)
     summed = pl.pallas_call(
         layer_kernel,
-        out_shape=jax.ShapeDtypeStruct((seqs, share, model), BF16),
-        in_specs=[pl.BlockSpec(memory_space=pltpu.HBM)] * 8,
+        out_shape=jax.ShapeDtypeStruct((share, seqs, model), F32),
+        in_specs=[pl.BlockSpec(memory_space=pltpu.HBM)] * 9,
         out_specs=pl.BlockSpec(memory_space=pltpu.VMEM),
         scratch_shapes=[
             tokens,
@@ -569,6 +616,7 @@
             pltpu.VMEM((1, heads), F32),
             pltpu.VMEM((heads,) + square, F32),
             pltpu.VMEM((1, width), F32),
+            pltpu.VMEM((1, seqs), jnp.int32),
             pltpu.VMEM((width, model), BF16),
             pltpu.VMEM((pairs, rows, 2 * HS), BF16),
             pltpu.VMEM((pairs, rows, 2 * HS), BF16),
@@ -576,8 +624,9 @@
             pltpu.VMEM((pairs, rows, HS), BF16),
             pltpu.VMEM((pairs, rows, HS), BF16),
             pltpu.VMEM((pairs, rows, HS), F32),
+            pltpu.VMEM((share, model), F32),
             pltpu.VMEM((HALF, HS, 2 * HS), F32),
-            pltpu.VMEM((2, HS, 2 * HS), F32),
+            pltpu.VMEM((3, HS, 2 * HS), F32),
             pltpu.VMEM((2,) + square, F32),
             pltpu.VMEM((HALF,) + square, F32),
             pltpu.VMEM((2,) + square, F32),
@@ -591,14 +640,16 @@
             pltpu.VMEM((seqs, rows // SLOTS, width), F32),
             pltpu.VMEM((seqs, parts, 2, share, cols), F32),
             pltpu.VMEM((seqs, parts, share, cols), F32),
-            dma((10,)),
+            dma((11,)),
             dma((pairs,)),
             dma((HALF,)),
             dma((HALF,)),
             dma((pairs,)),
-            dma((2,)),
+            dma((3,)),
             dma,
             dma,
+            dma,
+            dma((2,)),
             dma,
             dma((seqs, parts)),
             dma((seqs, parts)),
@@ -623,12 +674,10 @@
         head_rate.reshape(1, heads),
         init_state,
         norm_gain.reshape(1, width),
+        plan.reshape(1, seqs),
         out_proj,
     )
-    straight = plan[0] == 0
-    return jnp.stack(
-        [jnp.where(straight, summed[0], summed[1]), jnp.where(straight, summed[1], summed[0])], axis=1
-    )
+    return summed.astype(BF16)
 
 
 def solution(mesh):

time: 95.9 us -> 92.8 us (0.968); the launches traced: 94.5 us -> 92.7 us
  local copies, waits for them, and re-layouts: 1.34 us -> 0 us
  other arithmetic: 1.12 us -> 2.46 us
  Pallas kernels: 91.3 us -> 90.2 us
    convert_element_type x0 -> x1, other arithmetic: none -> 2.46 us  [per_device(): return summed.astype(BF16)]
    another operation x1 -> x0, local copies, waits for them, and re-layouts: 1.34 us -> none  [per_device(): jnp.stack([jnp.where(straight, summed[0], summed[1]), jnp.where(straight,...]
    pallas_call x1, Pallas kernels: 91.3 us -> 90.2 us  [per_device(): pl.pallas_call(layer_kernel, out_shape=jax.ShapeDtypeStruct((share, seqs,...]
    select_n x1 -> x0, other arithmetic: 1.07 us -> none  [per_device(): jnp.where(straight, summed[0], summed[1])]
where the time goes in v5:
time: 92.8 us; the launch traced here: 92.7 us
  Pallas kernels  90.2 us (97%)
  other arithmetic  2.46 us (3%)
    pallas_call x1, Pallas kernels, per_device(): pl.pallas_call(layer_kernel, out_shape=jax.ShapeDtypeStruct((share, seqs,...  90.2 us
    convert_element_type x1, other arithmetic, per_device(): return summed.astype(BF16)  2.46 us

profile of v5, /device:TPU:166, one launch (start us, length us, event | category | flops | bytes accessed | tf_op | source)
XLA Modules:
  0.0 92.7 jit_solution(8878427521040959411)
XLA Ops:
  0.0 90.2 %layer.1 = f32[32,2,4096]{2,1,0:T(2,128)} custom-call(bf16[2,256,512]{2,1,0:T(8,128)(2,1)} %q_hbm.1, bf16[2,256,512]{2,1,0:T(8,128)(2,1)} %k_hbm.1, bf16[2,256,512]{2,1,0:T(8,128)(2,1)} %v_hbm.1, f32[2,4,256]{2,1,0:T(4,128)} %gate_hbm.1, f32[1,4]{1,0:T(1,128)} %bitcast.4, f32[4,128,128]{2,1,0:T(8,128)} %init_hbm.1, f32[1,512]{1,0:T(1,128)} %bitcast.3, ...), custom_call_target="tpu_custom_call" | custom-call | tf_op jit(solution)/shard_map/layer/pallas_call | solution.py:606
  90.2 2.5 %convert_element_type.3 = bf16[32,2,4096]{2,1,0:T(2,128)(2,1)} convert(f32[32,2,4096]{2,1,0:T(2,128)} %layer.1) | non-fusion elementwise | flops 262144 | bytes 1572864 | tf_op jit(solution)/shard_map/convert_element_type | solution.py:680

commit v6 on v5

--- a/solution.py
+++ b/solution.py
@@ -235,7 +235,7 @@
         device_id_type=MESH,
     )
 
-    def scan(s):
+    def gather_maps(s):
         @pl.when(first if s == 0 else jnp.logical_not(first))
         def _():
             for i in range(SIDE):
@@ -266,7 +266,22 @@
                     map_copy(0, far_across).start()
                     map_copy(1, partner).start()
 
-            @pl.when(stage > 0)
+            for k in range(SIDE, HALF - 1):
+                recv[k] = after(recv[SIDE - 1], recv[k])
+            if s > 0:
+
+                @pl.when(stage == 1)
+                def _():
+                    copy_wait(chain.at[1], c_recv)
+                    enter[0] = chain[1]
+                    chain[0] = applied(total[0], enter[0])
+                    chain_copy(0, far_across).start()
+                    chain_copy(1, partner).start()
+
+    def give_states(s):
+        @pl.when(first if s == 0 else jnp.logical_not(first))
+        def _():
+            @pl.when(stage > (0 if s == 0 else 1))
             def _():
                 copy_wait(chain.at[1], c_recv)
                 enter[0] = chain[1]
@@ -278,25 +293,17 @@
                     copy_wait(total.at[2], m_recv)
                     enter[0] = applied(total[2], chain[1])
 
-            else:
-
-                @pl.when(stage == 1)
-                def _():
-                    chain[0] = applied(total[0], enter[0])
-                    chain_copy(0, far_across).start()
-                    chain_copy(1, partner).start()
-
             @pl.when(stage == 3)
             def _():
                 t_copy.wait_recv()
                 enter[0] = applied(total[1], enter[0])
 
-            enter[1] = applied(recv[SIDE - 1], enter[0])
+            wout[0] = enter[0]
+            wout[SIDE] = applied(recv[SIDE - 1], enter[0])
             for i in range(2):
                 g = lax.rem(x + i, 2)
-                wout[SIDE * g] = enter[g]
                 for k in range(1, SIDE):
-                    wout[SIDE * g + k] = applied(recv[SIDE * g + k - 1], enter[g])
+                    wout[SIDE * g + k] = applied(recv[SIDE * g + k - 1], enter[0])
                 for i2 in range(SIDE):
                     c = SIDE * g + lax.rem(y + i2, SIDE)
 
@@ -501,12 +508,14 @@
                 out_ref[:, 0, cols] = jnp.where(straight, other, value)
                 out_ref[:, 1, cols] = jnp.where(straight, value, other)
 
-    scan(0)
+    gather_maps(0)
+    give_states(0)
     outputs(0)
     far_rows(0)
-    scan(1)
+    gather_maps(1)
     nearest(0)
     forwards(0)
+    give_states(1)
     outputs(1)
     far_rows(1)
     nearest(1)

time: 92.8 us -> 92.6 us (level)
  no operation moved by 1% of the time
where the time goes in v6:
time: 92.6 us; the launch traced here: 92.5 us
  Pallas kernels  90 us (97%)
  other arithmetic  2.46 us (3%)
    pallas_call x1, Pallas kernels, per_device(): pl.pallas_call(layer_kernel, out_shape=jax.ShapeDtypeStruct((share, seqs,...  90 us
    convert_element_type x1, other arithmetic, per_device(): return summed.astype(BF16)  2.46 us

profile of v6, /device:TPU:166, one launch (start us, length us, event | category | flops | bytes accessed | tf_op | source)
XLA Modules:
  0.0 92.5 jit_solution(1600688041540252263)
XLA Ops:
  0.0 90.0 %layer.1 = f32[32,2,4096]{2,1,0:T(2,128)} custom-call(bf16[2,256,512]{2,1,0:T(8,128)(2,1)} %q_hbm.1, bf16[2,256,512]{2,1,0:T(8,128)(2,1)} %k_hbm.1, bf16[2,256,512]{2,1,0:T(8,128)(2,1)} %v_hbm.1, f32[2,4,256]{2,1,0:T(4,128)} %gate_hbm.1, f32[1,4]{1,0:T(1,128)} %bitcast.4, f32[4,128,128]{2,1,0:T(8,128)} %init_hbm.1, f32[1,512]{1,0:T(1,128)} %bitcast.3, ...), custom_call_target="tpu_custom_call" | custom-call | tf_op jit(solution)/shard_map/layer/pallas_call | solution.py:615
  90.0 2.5 %convert_element_type.3 = bf16[32,2,4096]{2,1,0:T(2,128)(2,1)} convert(f32[32,2,4096]{2,1,0:T(2,128)} %layer.1) | non-fusion elementwise | flops 262144 | bytes 1572864 | tf_op jit(solution)/shard_map/convert_element_type | solution.py:689
